TPU v7x, 128 devices: a whole 4x4x4 slice. The times are simulated.
128 devices in a mesh: grp: 16 (over y, x_lo, core), blk: 8 (over x_hi, z).
Axes of the slice: x: 4 (x_hi: 2, x_lo: 2; x = x_hi * 2 + x_lo), y: 4, z: 4, core: 2. Of those that a mesh axis runs over, the one named last changes fastest.
Arguments:
- queries: bfloat16 [16384, 4096], P(('grp', 'blk')), may hold values from -0.45 to 0.45
- passages: bfloat16 [16384, 4096], P(('grp', 'blk')), may hold values from -0.45 to 0.45
- positives: int32 [16, 1024], P('grp', 'blk'), may hold values from 0 to 1023, as said below
- hard_owner: int32 [16384, 3], P(('grp', 'blk')), may hold values from 0 to 127, all different within a row; in each aligned block of 128 rows (0 to 127, 128 to 255, ...) at most 4 rows name the same one
- hard_row: int32 [16384, 3], P(('grp', 'blk')), may hold values from 0 to 127
Outputs:
- loss: float32 [16384], P(('grp', 'blk'))
- grad_queries: float32 [16384, 4096], P(('grp', 'blk'))
- grad_passages: float32 [16384, 4096], P(('grp', 'blk'))
Inputs may be any that keep to these rules, and one draw needn't show every extreme that they name: `hard_owner`: within each aligned block of 128 rows (the queries of one device), no owner is named by more than 4 entries, a bound that some block reaches; the three owners of a row differ. Each row of positives is a permutation of 0 to 1023.
All inputs are finite; a program needn't handle non-finite values.
Results may differ from a plain program's by a relative error of at most 0.013.
Values may be sent and summed in bfloat16 or wider, within the bound.
A program may use at most 128 MiB of HBM per device.

v0:
```python
import math

import jax
import jax.numpy as jnp
from jax import lax
from jax.sharding import PartitionSpec as P

LOGIT_SCALE = 20.0


def on_device(queries, passages, positives, hard_owner, hard_row):
    rows = queries.shape[0]
    width = queries.shape[1]
    nblk = lax.axis_size("blk")
    ndev = lax.axis_size(("grp", "blk"))
    nhard = hard_owner.shape[1]
    slots_cap = max(2, (nhard * rows + ndev - 1) // ndev + 1)
    hard_shift = math.log(rows * nblk / nhard)
    pos = positives[0]
    owner_flat = hard_owner.reshape(-1)
    offset_flat = hard_row.reshape(-1)
    owner_hot = (owner_flat[:, None] == jnp.arange(ndev, dtype=jnp.int32)[None, :]).astype(
        jnp.int32
    )
    preceding_value = jnp.cumsum(owner_hot, axis=0) - owner_hot
    rank = jnp.sum(preceding_value * owner_hot, axis=1)
    slot = owner_flat * slots_cap + rank
    wanted = (
        jnp.zeros((ndev * slots_cap,), jnp.int32).at[slot].set(offset_flat).reshape(ndev, slots_cap)
    )
    asked = lax.all_to_all(wanted, ("grp", "blk"), split_axis=0, concat_axis=0, tiled=True)
    asked_flat = asked.reshape(-1)
    served = passages[asked_flat].reshape(ndev, slots_cap, width)
    fetched = lax.all_to_all(served, ("grp", "blk"), split_axis=0, concat_axis=0, tiled=True)
    hard = fetched.reshape(-1, width)[slot].reshape(rows, nhard, width)
    hard_scores = (
        jnp.einsum("qd,qkd->qk", queries, hard, preferred_element_type=jnp.float32) * LOGIT_SCALE
        + hard_shift
    )
    group = lax.all_gather(passages, "blk", axis=0, tiled=True)
    scores = jnp.dot(queries, group.T, preferred_element_type=jnp.float32) * LOGIT_SCALE
    top = jnp.maximum(jnp.max(scores, axis=1), jnp.max(hard_scores, axis=1))
    total = jnp.sum(jnp.exp(scores - top[:, None]), axis=1) + jnp.sum(
        jnp.exp(hard_scores - top[:, None]), axis=1
    )
    lse = top + jnp.log(total)
    columns = jnp.arange(group.shape[0], dtype=jnp.int32)
    indicator_vector = (columns[None, :] == pos[:, None]).astype(jnp.float32)
    loss = lse - jnp.sum(scores * indicator_vector, axis=1)
    coef = (jnp.exp(scores - lse[:, None]) - indicator_vector).astype(jnp.bfloat16)
    hard_coef = jnp.exp(hard_scores - lse[:, None])
    coefficient_block_list = coef.reshape(rows, nblk, rows)
    group_block_list = group.reshape(nblk, rows, width)
    parts = (
        jnp.einsum(
            "xay,ayn->axn",
            coefficient_block_list,
            group_block_list,
            preferred_element_type=jnp.float32,
        )
        * LOGIT_SCALE
    )
    grad_group_q = jnp.sum(parts.astype(jnp.bfloat16).astype(jnp.float32), axis=0)
    grad_group_p = lax.psum_scatter(
        (
            jnp.einsum("qj,qd->jd", coef, queries, preferred_element_type=jnp.float32) * LOGIT_SCALE
        ).astype(jnp.bfloat16),
        "blk",
        scatter_dimension=0,
        tiled=True,
    ).astype(jnp.float32)
    grad_queries = grad_group_q + LOGIT_SCALE * jnp.einsum(
        "qk,qkd->qd", hard_coef, hard, preferred_element_type=jnp.float32
    )
    hard_part = (
        LOGIT_SCALE * hard_coef[:, :, None] * queries[:, None, :].astype(jnp.float32)
    ).astype(jnp.bfloat16)
    outgoing = (
        jnp.zeros((ndev * slots_cap, width), jnp.bfloat16)
        .at[slot]
        .set(hard_part.reshape(-1, width))
    )
    arrived = lax.all_to_all(
        outgoing.reshape(ndev, slots_cap, width),
        ("grp", "blk"),
        split_axis=0,
        concat_axis=0,
        tiled=True,
    )
    row_hot = (asked_flat[:, None] == jnp.arange(rows, dtype=jnp.int32)[None, :]).astype(
        jnp.bfloat16
    )
    hard_sum_rows = jnp.einsum(
        "sj,sd->jd", row_hot, arrived.reshape(-1, width), preferred_element_type=jnp.float32
    )
    grad_passages = grad_group_p + hard_sum_rows
    return (loss, grad_queries, grad_passages)


def solution(mesh):
    return jax.shard_map(
        on_device,
        mesh=mesh,
        in_specs=(
            P(("grp", "blk"), None),
            P(("grp", "blk"), None),
            P("grp", "blk"),
            P(("grp", "blk"), None),
            P(("grp", "blk"), None),
        ),
        out_specs=(P(("grp", "blk")), P(("grp", "blk"), None), P(("grp", "blk"), None)),
        check_vma=False,
    )
```

profile of v0, /device:TPU:1, one launch (start us, length us, event | category | flops | bytes accessed | tf_op | source)
XLA Modules:
  0.0 368.3 jit_solution(7479917259044692271)
XLA Ops:
  7.2 0.7 all-gather.2.cloned.1.call-update
  7.9 0.8 copy.17
  8.7 0.2 eq.59
  8.9 0.2 eq.55
  9.1 0.7 broadcast_multiply_fusion.1
  9.8 0.1 copy.16
  9.9 0.2 mul.79
  10.1 0.1 copy.19
  10.2 0.2 fusion.8
  10.5 0.1 broadcast_add_fusion
  10.6 0.8 copy.21
  11.4 0.2 reshape.169
  11.6 0.2 fusion.11
  11.8 2.9 scatter_custom_fusion
  14.8 0.1 all_to_all.12
  14.9 21.4 %all_to_all.19 = s32[128,1,4]{2,1,0:T(1,128)S(1)} all-to-all(s32[128,1,4]{2,1,0:T(1,128)S(1)} %bitcast.47), channel_id=1, replica_groups=mesh['grp'=16,'blk'=8] {'grp','blk'}, dimensions={0} | all-to-all | bytes 4096 | tf_op jit(solution)/shard_map/all_to_all | solution.py:31
  36.2 0.5 broadcast.98
  36.7 0.8 reduce.7
  37.5 0.1 reshape.141
  37.7 4.4 %gather_fusion = bf16[512,4096]{1,0:T(8,128)(2,1)} fusion(bf16[128,4096]{1,0:T(8,128)(2,1)S(1)} %copy-done, s32[1024]{0:T(1024)S(1)} %pad_clamp_fusion.1), kind=kCustom, calls=%fused_computation | custom fusion | bytes 8390656 | tf_op jit(solution)/shard_map/gather | solution.py:33
  42.0 7.2 %reshape.142 = bf16[128,4,4096]{2,1,0:T(4,128)(2,1)} reshape(bf16[512,4096]{1,0:T(8,128)(2,1)} %gather_fusion) | data formatting | bytes 8388608 | tf_op jit(solution)/shard_map/reshape | solution.py:33
  49.2 11.9 %all-to-all-start.1 = ((bf16[128,4,4096]{2,1,0:T(4,128)(2,1)}), bf16[128,4,4096]{2,1,0:T(4,128)(2,1)}, u32[]{:S(2)}, u32[]{:S(2)}) async-start(bf16[128,4,4096]{2,1,0:T(4,128)(2,1)} %reshape.142), calls=%async_computation.1 | async-start | bytes 8388608 | tf_op jit(solution)/shard_map/all_to_all | solution.py:34
  61.2 93.2 %all-to-all-done.1 = bf16[128,4,4096]{2,1,0:T(4,128)(2,1)} async-done(((bf16[128,4,4096]{2,1,0:T(4,128)(2,1)}), bf16[128,4,4096]{2,1,0:T(4,128)(2,1)}, u32[]{:S(2)}, u32[]{:S(2)}) %all-to-all-start.1) | async-done | bytes 4194336 | tf_op jit(solution)/shard_map/all_to_all | solution.py:34
  154.5 6.9 %reshape.143 = bf16[512,4096]{1,0:T(8,128)(2,1)} reshape(bf16[128,4,4096]{2,1,0:T(4,128)(2,1)} %all-to-all-done.1) | data formatting | bytes 8388608 | tf_op jit(solution)/shard_map/reshape | solution.py:35
  161.4 10.2 %gather_fusion.1 = bf16[384,4096]{1,0:T(8,128)(2,1)S(1)} fusion(bf16[512,4096]{1,0:T(8,128)(2,1)} %reshape.143, s32[1024]{0:T(1024)S(1)} %pad_clamp_fusion), kind=kCustom, calls=%fused_computation.1 | custom fusion | bytes 6292992 | tf_op jit(solution)/shard_map/gather | solution.py:35
  171.6 4.4 %reshape.144 = bf16[128,3,4096]{2,1,0:T(4,128)(2,1)} reshape(bf16[384,4096]{1,0:T(8,128)(2,1)S(1)} %gather_fusion.1) | data formatting | bytes 6291456 | tf_op jit(solution)/shard_map/reshape | solution.py:35
  176.0 8.1 %fusion.4 = f32[128,1,3]{2,1,0:T(1,128)S(1)} fusion(bf16[128,3,4096]{2,1,0:T(4,128)(2,1)} %reshape.144, bf16[128,4096,1]{1,0,2:T(8,128)(2,1)} %bitcast.41), kind=kOutput, calls=%fused_computation.14 | convolution fusion | flops 3145728 | bytes 4195840 | tf_op jit(solution)/shard_map/qd,qkd->qk/dot_general | solution.py:37
  184.1 0.1 fusion.14
  184.3 6.3 %fusion.20 = (f32[128]{0:T(128)S(1)}, f32[128,1024]{1,0:T(8,128)S(1)}) fusion(bf16[128,4096]{1,0:T(8,128)(2,1)S(1)} %copy-done.1, bf16[1024,4096]{1,0:T(8,128)(2,1)} %all-gather.2.cloned.1.call-done), kind=kOutput, calls=%fused_computation.51 | convolution fusion | flops 1074003840 | bytes 9961984 | tf_op jit(solution)/shard_map/dot_general | solution.py:41
  190.6 0.2 exponential_reduce_fusion.1
  190.8 0.3 select_reduce_fusion
  191.1 0.5 fusion.19
  191.6 5.7 %multiply_convert_fusion = bf16[1024,4096]{1,0:T(8,128)(2,1)} fusion(bf16[128,4096]{1,0:T(8,128)(2,1)S(1)} %copy-done.1, f32[128,1024]{1,0:T(8,128)S(1)} %get-tuple-element.10, f32[128]{0:T(128)S(1)} %get-tuple-element.8, s32[128]{0:T(128)S(1)} %bitcast.52), kind=kOutput, calls=%fused_computation.4 | convolution fusion | flops 1082785792 | bytes 9962496 | tf_op jit(solution)/shard_map/qj,qd->jd/dot_general | solution.py:66
  197.4 5.3 %mul.93 = f32[128,3,4096]{2,1,0:T(4,128)} broadcast(bf16[128,4096]{1,0:T(8,128)(2,1)S(1)} %copy-done.1), dimensions={0,2} | broadcast | bytes 7340032 | tf_op jit(solution)/shard_map/mul | solution.py:76
  202.7 9.2 %mul.94 = f32[384,4096]{1,0:T(8,128)} reshape(f32[128,3,4096]{2,1,0:T(4,128)} %mul.93) | data formatting | bytes 12582912 | tf_op jit(solution)/shard_map/mul | solution.py:76
  211.9 0.1 broadcast_multiply_fusion
  212.0 0.2 mul.91
  212.2 9.9 %scatter_custom_fusion.1 = bf16[512,4096]{1,0:T(8,128)(2,1)} fusion(s32[384]{0:T(512)S(1)} %fusion.15, f32[384,4096]{1,0:T(8,128)} %mul.94, f32[384]{0:T(512)S(1)} %mul.91, bf16[]{:T(256)} %constant.4.clone.1), kind=kCustom, calls=%fused_computation.9 | custom fusion | flops 3145728 | bytes 10487810 | tf_op jit(solution)/shard_map/scatter | solution.py:81
  222.1 7.3 %reshape.147 = bf16[128,4,4096]{2,1,0:T(4,128)(2,1)} reshape(bf16[512,4096]{1,0:T(8,128)(2,1)} %scatter_custom_fusion.1) | data formatting | bytes 8388608 | tf_op jit(solution)/shard_map/reshape | solution.py:84
  229.4 6.9 %all-to-all-start.2 = ((bf16[128,4,4096]{2,1,0:T(4,128)(2,1)}), bf16[128,4,4096]{2,1,0:T(4,128)(2,1)}, u32[]{:S(2)}, u32[]{:S(2)}) async-start(bf16[128,4,4096]{2,1,0:T(4,128)(2,1)} %reshape.147), calls=%async_computation.3 | async-start | bytes 8388608 | tf_op jit(solution)/shard_map/all_to_all | solution.py:83
  236.3 0.1 eq.67
  236.4 4.6 %fusion.21 = f32[128,1,4096]{2,1,0:T(1,128)S(1)} fusion(f32[128,3,1]{1,2,0:T(1,128)S(1)} %bitcast.48, bf16[128,3,4096]{2,1,0:T(4,128)(2,1)} %reshape.144), kind=kOutput, calls=%fused_computation.52 | convolution fusion | flops 3145728 | bytes 5244416 | tf_op jit(solution)/shard_map/qk,qkd->qd/dot_general | solution.py:72
  241.0 6.1 %convert_reduce_fusion = f32[128,4096]{1,0:T(8,128)S(1)} fusion(bf16[8,128,4096]{2,1,0:T(8,128)(2,1)} %bitcast.42, s32[128]{0:T(128)S(1)} %bitcast.53, f32[128,1024]{1,0:T(8,128)S(1)} %get-tuple-element.10, f32[128]{0:T(128)S(1)} %get-tuple-element.8), kind=kOutput, calls=%fused_computation.5 | convolution fusion | flops 1090650112 | bytes 11011072 | tf_op jit(solution)/shard_map/xay,ayn->axn/dot_general | solution.py:55
  247.1 3.3 fusion.2
  250.3 37.1 %all-to-all-done.2 = bf16[128,4,4096]{2,1,0:T(4,128)(2,1)} async-done(((bf16[128,4,4096]{2,1,0:T(4,128)(2,1)}), bf16[128,4,4096]{2,1,0:T(4,128)(2,1)}, u32[]{:S(2)}, u32[]{:S(2)}) %all-to-all-start.2) | async-done | bytes 4194336 | tf_op jit(solution)/shard_map/all_to_all | solution.py:83
  287.4 7.0 %reshape.148 = bf16[512,4096]{1,0:T(8,128)(2,1)} reshape(bf16[128,4,4096]{2,1,0:T(4,128)(2,1)} %all-to-all-done.2) | data formatting | bytes 8388608 | tf_op jit(solution)/shard_map/reshape | solution.py:94
  294.4 62.3 %reduce-scatter.2.cloned.1.call-done = bf16[128,4096]{1,0:T(8,128)(2,1)} async-done(((bf16[1024,4096]{1,0:T(8,128)(2,1)}), bf16[128,4096]{1,0:T(8,128)(2,1)}) %reduce-scatter.2.cloned.1.call-update) | async-done | bytes 1048592 | tf_op jit(solution)/shard_map/reduce_scatter | solution.py:64
  356.8 4.6 %convolution_add_fusion = f32[128,4096]{1,0:T(8,128)} fusion(bf16[512,4096]{1,0:T(8,128)(2,1)} %reshape.148, bf16[128,4096]{1,0:T(8,128)(2,1)} %reduce-scatter.2.cloned.1.call-done, s32[512]{0:T(512)S(1)} %eq.67), kind=kOutput, calls=%fused_computation.8 | convolution fusion | flops 537985024 | bytes 7342080 | tf_op jit(solution)/shard_map/sj,sd->jd/dot_general | solution.py:93
  (18 shorter events, 0.2 us)
Async XLA Ops:
  7.2 30.5 %copy-start = (bf16[128,4096]{1,0:T(8,128)(2,1)S(1)}, bf16[128,4096]{1,0:T(8,128)(2,1)}, u32[]{:S(2)}) copy-start(bf16[128,4096]{1,0:T(8,128)(2,1)} %param.6) | copy-start | bytes 3145732
  7.2 177.1 %all-gather.2.cloned.1.call-start = ((), (), s32[]{:S(2)}) async-start(), calls=%async_computation.4 | async-start | bytes 9437184 | tf_op jit(solution)/shard_map/all_gather | solution.py:40
  49.2 105.2 %all-to-all-start.1 = ((bf16[128,4,4096]{2,1,0:T(4,128)(2,1)}), bf16[128,4,4096]{2,1,0:T(4,128)(2,1)}, u32[]{:S(2)}, u32[]{:S(2)}) async-start(bf16[128,4,4096]{2,1,0:T(4,128)(2,1)} %reshape.142), calls=%async_computation.1 | async-start | bytes 8388608 | tf_op jit(solution)/shard_map/all_to_all | solution.py:34
  61.2 295.6 %reduce-scatter.2.cloned.1.call-start = ((), (), s32[]{:S(2)}) async-start(), calls=%async_computation.5 | async-start | bytes 9437184 | tf_op jit(solution)/shard_map/reduce_scatter | solution.py:64
  176.0 8.3 %copy-start.1 = (bf16[128,4096]{1,0:T(8,128)(2,1)S(1)}, bf16[128,4096]{1,0:T(8,128)(2,1)}, u32[]{:S(2)}) copy-start(bf16[128,4096]{1,0:T(8,128)(2,1)} %param.5) | copy-start | bytes 3145732
  184.2 6.6 %copy-start.2 = (s32[1,128]{1,0:T(1,128)S(1)}, s32[1,128]{1,0:T(1,128)}, u32[]{:S(2)}) copy-start(s32[1,128]{1,0:T(1,128)} %param.7) | copy-start | bytes 1540
  229.4 58.0 %all-to-all-start.2 = ((bf16[128,4,4096]{2,1,0:T(4,128)(2,1)}), bf16[128,4,4096]{2,1,0:T(4,128)(2,1)}, u32[]{:S(2)}, u32[]{:S(2)}) async-start(bf16[128,4,4096]{2,1,0:T(4,128)(2,1)} %reshape.147), calls=%async_computation.3 | async-start | bytes 8388608 | tf_op jit(solution)/shard_map/all_to_all | solution.py:83
Sparse Core Ops, SparseCore 0:
  10.4 153.0 all-gather.1
  197.5 159.2 reduce-scatter.1
where the time goes:
time: 370 us; the launch traced here: 368 us
  waiting for transfers between devices  193 us (52%)
  local copies, waits for them, and re-layouts  68.6 us (19%)
  matrix products  35.4 us (10%)
  blocking collectives  21.4 us (6%)
  starting transfers between devices  18.9 us (5%)
  other arithmetic  16.4 us (4%)
  between operations  14.2 us (4%)
    all_to_all x1, waiting for transfers between devices, on_device(): lax.all_to_all(served, ('grp', 'blk'), split_axis=0, concat_axis=0, tiled...  93.2 us
    reduce_scatter x1, waiting for transfers between devices, on_device(): lax.psum_scatter((jnp.einsum('qj,qd->jd', coef, queries, preferred_elemen...  62.3 us
    all_to_all x1, waiting for transfers between devices, on_device(): lax.all_to_all(outgoing.reshape(ndev, slots_cap, width), ('grp', 'blk'),...  37.1 us
    all_to_all x1, blocking collectives, on_device(): lax.all_to_all(wanted, ('grp', 'blk'), split_axis=0, concat_axis=0, tiled...  21.4 us
    mul x3, local copies, waits for them, and re-layouts, on_device(): LOGIT_SCALE * hard_coef[:, :, None]  14.8 us
    all_to_all x1, starting transfers between devices, on_device(): lax.all_to_all(served, ('grp', 'blk'), split_axis=0, concat_axis=0, tiled...  11.9 us
    reshape x2, local copies, waits for them, and re-layouts, on_device(): hard = fetched.reshape(-1, width)[slot].reshape(rows, nhard, width)  11.3 us
    gather x1, local copies, waits for them, and re-layouts, on_device(): hard = fetched.reshape(-1, width)[slot].reshape(rows, nhard, width)  10.2 us
  transfers between devices with their start and end apart: 4, of which 3 were waited for; matrix products, arithmetic and copies ran while one was open for 28% of the time, Pallas kernels for 0%

commit v1 on v0

v1 whole, which is shorter than its diff:
```python
import functools
import math

import jax
import jax.numpy as jnp
from jax import lax
from jax.experimental import pallas as pl
from jax.experimental.pallas import tpu as pltpu
from jax.sharding import PartitionSpec as P

LOGIT_SCALE = 20.0
ROWS = 128
CAP = 4
NCH = 4
NEG = -1e30
MESH = pl.DeviceIdType.MESH
F32 = jnp.float32
BF16 = jnp.bfloat16


def iota(shape, dim):
    return lax.broadcasted_iota(jnp.int32, shape, dim)


def to_column(row):
    n = row.shape[1]
    eye = iota((n, n), 0) == iota((n, n), 1)
    return jnp.sum(jnp.where(eye, row, jnp.zeros_like(row)), axis=1, keepdims=True)


def to_row(col):
    n = col.shape[0]
    eye = iota((n, n), 0) == iota((n, n), 1)
    return jnp.sum(jnp.where(eye, col, jnp.zeros_like(col)), axis=0, keepdims=True)


def mm(a, b):
    return jnp.dot(a, b, preferred_element_type=F32)


def mm_t(a, b):
    return lax.dot_general(a, b, (((1,), (1,)), ((), ())), preferred_element_type=F32)


def kernel(
    NY, NC, D, shift,
    q_hbm, p_hbm, pos_ref, own_ref, row_ref,
    loss_ref, gq_ref, gp_ref,
    PZ, QX, SP, SQ, RP, RQ,
    rs_a, rs_up, rs_dn, rr_a, rr_up, rr_dn, gx_s, gx_r,
    s_own, s_par, hs, gather, coef_o, coef_p, coef_t, hmat,
    xt_s, xt_r, w_s, w_r, j_s, j_r, cx_s, cx_r, c_s, c_r, st_s, st_r, lse_s, lse_r,
    in_sem, ag_send, ag_recv, hard_send, hard_recv,
    xt_send, xt_recv, cx_send, cx_recv, small_send, small_recv, pair_send, pair_recv, rs_send, rs_recv,
):
    R = 4 * NY * NC
    S = 16 * R
    DC = D // NCH
    H = DC // 2
    HD = D // 2
    TN = min(512, H)
    g = lax.axis_index("grp")
    b = lax.axis_index("blk")
    z = lax.rem(b, 4)
    xh = b // 4
    c = lax.rem(g, NC)
    x = xh * 2 + lax.rem(g // NC, 2)
    y = g // (2 * NC)

    def dev(dx, dy, dz, dc):
        x2 = lax.rem(x + dx, 4)
        y2 = lax.rem(y + dy, NY)
        z2 = lax.rem(z + dz, 4)
        c2 = lax.rem(c + dc, NC)
        return ((y2 * 2 + lax.rem(x2, 2)) * NC + c2, (x2 // 2) * 4 + z2)

    def order(n):
        cc = lax.rem(n, NC)
        i = lax.rem(n // NC, 4)
        s = n // (4 * NC)
        a = lax.rem(1 + 2 * i + i // 2, 4)
        yy = lax.rem(a + s + 1, NY)
        return a, yy, cc, (a * NY + yy) * NC + cc

    p_in = pltpu.make_async_copy(p_hbm, PZ.at[pl.ds(z * ROWS, ROWS)], in_sem.at[0])
    q_in = pltpu.make_async_copy(q_hbm, QX.at[pl.ds(x * ROWS, ROWS)], in_sem.at[1])
    p_in.start()
    q_in.start()
    barrier = pltpu.get_barrier_semaphore()

    def greet(n, carry):
        a, yy, cc, r = order(n)

        @pl.when(r > 0)
        def _():
            pl.semaphore_signal(barrier, inc=1, device_id=dev(a, yy, 0, cc), device_id_type=MESH)

        @pl.when(a > 0)
        def _():
            pl.semaphore_signal(barrier, inc=1, device_id=dev(0, yy, a, cc), device_id_type=MESH)

        return carry

    lax.fori_loop(0, R, greet, 0)
    pl.semaphore_wait(barrier, (R - 1) + 3 * NY * NC)
    p_in.wait()
    q_in.wait()

    def block(buf, i, col, width):
        return buf.at[pl.ds(lax.rem(i + 4, 4) * ROWS, ROWS), pl.ds(col, width)]

    def ring(which, kind, ch):
        buf, me = ((PZ, z), (QX, x))[which]
        step = 1 if kind in (0, 2) else 3
        blk = me if kind < 2 else (me - 1 if kind == 2 else me + 1)
        col = ch * DC + (H if kind == 3 else 0)
        width = DC if kind < 2 else H
        ref = block(buf, blk, col, width)
        target = dev(0, 0, step, 0) if which == 0 else dev(step, 0, 0, 0)
        return pltpu.make_async_remote_copy(
            ref, ref, ag_send.at[which, kind, ch], ag_recv.at[which, kind, ch],
            device_id=target, device_id_type=MESH,
        )

    def arriving(which, kind, ch):
        buf, me = ((PZ, z), (QX, x))[which]
        blk = (me - 1, me + 1, me - 2, me + 2)[kind]
        col = ch * DC + (H if kind == 3 else 0)
        width = DC if kind < 2 else H
        ref = block(buf, blk, col, width)
        return pltpu.make_async_remote_copy(
            ref, ref, ag_send.at[which, kind, ch], ag_recv.at[which, kind, ch],
            device_id=dev(0, 0, 1, 0), device_id_type=MESH,
        )

    def own_sends(ch):
        for which in (0, 1):
            ring(which, 0, ch).start()
            ring(which, 1, ch).start()

    own_sends(0)
    own_sends(1)

    lane = iota((1, S), 1)
    slot_r = lane // 16
    slot_b = lax.rem(lane, 16) // 4
    slot_t = lax.rem(lane, 4)
    r_a = slot_r // (NY * NC)
    r_y = lax.rem(slot_r // NC, NY)
    r_c = lax.rem(slot_r, NC)

    def dev_id(x2, y2, z2, c2):
        return ((y2 * 2 + lax.rem(x2, 2)) * NC + c2) * 8 + (x2 // 2) * 4 + z2

    owner = own_ref[...]
    hrow = row_ref[...].astype(F32)
    ndev = 8 * 2 * NY * NC
    width = max(ndev, 128)
    lane_o = iota((ROWS, width), 1)
    hot = [(owner[:, k : k + 1] == lane_o).astype(F32) for k in range(3)]
    count = hot[0] + hot[1] + hot[2]
    lower = (iota((ROWS, ROWS), 1) < iota((ROWS, ROWS), 0)).astype(BF16)
    before = mm(lower, count.astype(BF16))
    rank = [jnp.sum(h * before, axis=1, keepdims=True).astype(jnp.int32) for h in hot]

    def code(k):
        return owner[:, k : k + 1] * CAP + rank[k]

    codes = [jnp.where(owner[:, k : k + 1] >= 0, code(k), -1) for k in range(3)]
    codes_p = (
        dev_id(lax.rem(x + 4 - r_a, 4), lax.rem(y + NY - r_y, NY), slot_b, lax.rem(c + NC - r_c, NC)) * CAP + slot_t
    )

    def codes_q(dx):
        full = dev_id(lax.rem(x + dx, 4), lax.rem(y + r_y, NY), lax.rem(z + r_a, 4), lax.rem(c + r_c, NC)) * CAP + slot_t
        return jnp.where(slot_b == x, full, -2)

    def pick(code_row, values):
        total = jnp.zeros((ROWS, S), F32)
        for k in range(3):
            total = total + jnp.where(codes[k] == code_row, values[k], 0.0)
        return jnp.sum(total, axis=0, keepdims=True)

    rows_k = [hrow[:, k : k + 1] for k in range(3)]
    w_row = pick(codes_p, rows_k)
    w_s[0] = w_row
    w_r[0] = w_row

    def spread(kind, src, dst, wide):
        def body(n, carry):
            a, yy, cc, r = order(n)

            @pl.when(r > 0)
            def _():
                neg = (lax.rem(4 - a, 4), lax.rem(NY - yy, NY), lax.rem(NC - cc, NC))
                target = dev(neg[0], neg[1], 0, neg[2]) if kind == 0 else dev(0, yy, a, cc)
                pltpu.make_async_remote_copy(
                    src.at[0], dst.at[r], small_send.at[wide], small_recv.at[wide],
                    device_id=target, device_id_type=MESH,
                ).start()

            return carry

        lax.fori_loop(0, R, body, 0)

    def spread_all(dst, wide):
        return pltpu.make_async_remote_copy(
            dst.at[pl.ds(1, R - 1)], dst.at[pl.ds(1, R - 1)], small_send.at[wide], small_recv.at[wide],
            device_id=dev(1, 0, 0, 0), device_id_type=MESH,
        )

    def fold(ref):
        values = ref[...]
        keep = iota((R, 1, S), 2) // 16 == iota((R, 1, S), 0)
        return jnp.sum(jnp.where(keep, values, 0.0), axis=0)

    spread(0, w_s, w_r, 0)

    query_number = iota((ROWS, 1), 0).astype(F32)
    pos_row = pos_ref[...].astype(F32)
    pos_wide = jnp.concatenate([pos_row] + [jnp.zeros((1, S - ROWS), F32)], axis=1)
    sub8 = iota((8, S), 0)
    for dx in range(4):
        cq = codes_q(dx)
        v_row = pick(cq, [query_number] * 3)
        jj_row = pick(cq, rows_k)
        table = jnp.where(sub8 == 0, v_row, 0.0) + jnp.where(sub8 == 1, jj_row, 0.0) + jnp.where(sub8 == 2, pos_wide, 0.0)
        xt_s[dx] = table
        if dx == 0:
            xt_r[0] = table

    def x_peer(src, dst, send, recv, dx):
        return pltpu.make_async_remote_copy(
            src.at[dx], dst.at[dx], send.at[dx], recv.at[dx], device_id=dev(dx, 0, 0, 0), device_id_type=MESH
        )

    for dx in range(1, 4):
        x_peer(xt_s, xt_r, xt_send, xt_recv, dx).start()
    for dx in range(1, 4):
        x_peer(xt_s, xt_r, xt_send, xt_recv, dx).wait_recv()
    tables = xt_r[0] + xt_r[1] + xt_r[2] + xt_r[3]
    v_all = tables[0:1, :]
    j_s[0] = tables[1:2, :]
    j_r[0] = tables[1:2, :]
    spread(1, j_s, j_r, 1)

    def gather_matrix(index, slot):
        n = iota((S, 1), 0)
        want = to_column(index).astype(jnp.int32) + lax.rem(n, 16) // 4 * ROWS
        gather[slot] = (want == iota((S, 4 * ROWS), 1)).astype(BF16)

    spread_all(w_r, 0).wait_recv()
    gather_matrix(fold(w_r), 0)
    gather_matrix(v_all, 1)

    def hard_starts(kind, ch):
        src, dst = ((SP, RP), (SQ, RQ))[kind]

        def body(n, carry):
            a, yy, cc, r = order(n)

            @pl.when(r > 0)
            def _():
                target = dev(a, yy, 0, cc) if kind == 0 else dev(0, yy, a, cc)
                pltpu.make_async_remote_copy(
                    src.at[pl.ds(r * 16, 16), pl.ds(ch * DC, DC)], dst.at[pl.ds(r * 16, 16), pl.ds(ch * DC, DC)],
                    hard_send.at[kind, ch], hard_recv.at[kind, ch], device_id=target, device_id_type=MESH,
                ).start()

            return carry

        lax.fori_loop(0, R, body, 0)

    def hard_all(kind, ch):
        src, dst = ((SP, RP), (SQ, RQ))[kind]
        ref = lambda buf: buf.at[pl.ds(16, S - 16), pl.ds(ch * DC, DC)]
        return pltpu.make_async_remote_copy(
            ref(src), ref(dst), hard_send.at[kind, ch], hard_recv.at[kind, ch],
            device_id=dev(1, 0, 0, 0), device_id_type=MESH,
        )

    def tiles(start, length, body):
        def step(t, carry):
            body(pl.ds(pl.multiple_of(start + t * TN, 128), TN))
            return carry

        lax.fori_loop(0, length // TN, step, 0)

    def serve(kind, ch):
        src, out, mine = ((PZ, SP, RP), (QX, SQ, RQ))[kind]

        def body(cols):
            rows = mm(gather[kind], src[:, cols]).astype(BF16)
            out[:, cols] = rows
            mine[0:16, cols] = rows[0:16]

        tiles(ch * DC, DC, body)

    me_rows = pl.ds(x * ROWS, ROWS)
    par_rows = pl.ds(lax.rem(x + 2, 4) * ROWS, ROWS)
    s_own[...] = jnp.zeros_like(s_own)
    s_par[...] = jnp.zeros_like(s_par)
    hs[...] = jnp.zeros_like(hs)

    def score(acc, rows, keys, ch):
        def body(cols):
            acc[...] += mm_t(QX[rows, cols], keys[:, cols])

        tiles(ch * DC, DC, body)

    for ch in range(NCH):
        for which in (0, 1):
            for kind in (0, 1):
                arriving(which, kind, ch).wait_recv()
                ring(which, kind + 2, ch).start()
        if ch + 2 < NCH:
            own_sends(ch + 2)
        arriving(0, 2, ch).wait_recv()
        arriving(0, 3, ch).wait_recv()
        serve(0, ch)
        hard_starts(0, ch)
        score(s_own, me_rows, PZ, ch)
    for ch in range(NCH):
        arriving(1, 2, ch).wait_recv()
        arriving(1, 3, ch).wait_recv()
        serve(1, ch)
        hard_starts(1, ch)
    for ch in range(NCH):
        score(s_par, par_rows, PZ, ch)

    base = (xh * 4 * ROWS).astype(F32)
    lane_p = iota((ROWS, 4 * ROWS), 1).astype(F32)
    pos_own = to_column(pos_row) - base
    pos_par = to_column(xt_r[2][2:3, 0:ROWS]) - base

    def half_stats(acc, pos):
        s = acc[...] * LOGIT_SCALE
        m = jnp.max(s, axis=1, keepdims=True)
        l = jnp.sum(jnp.exp(s - m), axis=1, keepdims=True)
        sp = jnp.sum(jnp.where(lane_p == pos, s, 0.0), axis=1, keepdims=True)
        return m, l, sp

    lane128 = iota((ROWS, 128), 1)
    m_p, l_p, sp_p = half_stats(s_par, pos_par)
    st_s[...] = jnp.where(lane128 == 0, m_p, jnp.where(lane128 == 1, l_p, jnp.where(lane128 == 2, sp_p, 0.0)))

    def pair(src, dst, i):
        return pltpu.make_async_remote_copy(
            src, dst, pair_send.at[i], pair_recv.at[i], device_id=dev(2, 0, 0, 0), device_id_type=MESH
        )

    pair(st_s, st_r, 0).start()
    m_o, l_o, sp_o = half_stats(s_own, pos_own)

    for ch in range(NCH):
        hard_all(0, ch).wait_recv()
        score(hs, me_rows, RP, ch)
    pair(st_s, st_r, 0).wait_recv()
    stats = st_r[...]
    m_r, l_r, sp_r = stats[:, 0:1], stats[:, 1:2], stats[:, 2:3]
    scaled = hs[...] * LOGIT_SCALE + shift
    mask = [codes[k] == codes_p for k in range(3)]
    hard_k = [jnp.sum(jnp.where(mask[k], scaled, 0.0), axis=1, keepdims=True) for k in range(3)]
    present = [jnp.where(owner[:, k : k + 1] >= 0, hard_k[k], NEG) for k in range(3)]
    top = jnp.maximum(jnp.maximum(m_o, m_r), jnp.maximum(jnp.maximum(present[0], present[1]), present[2]))
    total = l_o * jnp.exp(m_o - top) + l_r * jnp.exp(m_r - top)
    for k in range(3):
        total = total + jnp.exp(present[k] - top)
    lse = top + jnp.log(total)
    lse_s[...] = jnp.broadcast_to(lse, (ROWS, 128))
    pair(lse_s, lse_r, 1).start()
    loss_ref[...] = to_row(lse - (sp_o + sp_r))
    hard_coef = [jnp.exp(present[k] - lse) for k in range(3)]

    for dx in range(4):
        row = pick(codes_q(dx), hard_coef)
        cx_s[dx] = row
        if dx == 0:
            cx_r[0] = row
    for dx in range(1, 4):
        x_peer(cx_s, cx_r, cx_send, cx_recv, dx).start()

    def half_coef(acc, pos, row_lse, out, column):
        f = jnp.exp(acc[...] * LOGIT_SCALE - row_lse) - jnp.where(lane_p == pos, 1.0, 0.0)
        out[...] = f.astype(BF16)
        coef_t[:, column * ROWS : (column + 1) * ROWS] = jnp.transpose(f).astype(BF16)

    half_coef(s_own, pos_own, lse, coef_o, 0)
    pair(lse_s, lse_r, 1).wait_recv()
    half_coef(s_par, pos_par, lse_r[:, 0:1], coef_p, 1)

    def passage_part(offset, cols):
        ct = coef_t[pl.ds(lax.rem(z + offset, 4) * ROWS, ROWS), :]
        part = mm(ct[:, 0:ROWS], QX[me_rows, cols]) + mm(ct[:, ROWS : 2 * ROWS], QX[par_rows, cols])
        return part * LOGIT_SCALE

    def rs(src, dst, i, step, start, length):
        return pltpu.make_async_remote_copy(
            src.at[:, pl.ds(start, length)], dst.at[:, pl.ds(start, length)], rs_send.at[i], rs_recv.at[i],
            device_id=dev(0, 0, step, 0), device_id_type=MESH,
        )

    far_up = rs(rs_a, rr_a, 0, 1, 0, HD)
    far_dn = rs(rs_a, rr_a, 1, 3, HD, HD)
    up_free = rs(rs_up, rr_up, 2, 1, HD, HD)
    dn_free = rs(rs_dn, rr_dn, 3, 3, 0, HD)
    up_last = rs(rs_up, rr_up, 4, 1, 0, HD)
    dn_last = rs(rs_dn, rr_dn, 5, 3, HD, HD)

    def far(cols):
        rs_a[:, cols] = passage_part(2, cols).astype(BF16)

    tiles(0, HD, far)
    far_up.start()
    tiles(HD, HD, far)
    far_dn.start()

    def partner_part(cols):
        gx_s[:, cols] = (mm(coef_p[...], PZ[:, cols]) * LOGIT_SCALE).astype(BF16)

    tiles(0, D, partner_part)
    pair(gx_s, gx_r, 2).start()

    def up_part(cols):
        rs_up[:, cols] = passage_part(1, cols).astype(BF16)

    def dn_part(cols):
        rs_dn[:, cols] = passage_part(3, cols).astype(BF16)

    tiles(HD, HD, up_part)
    up_free.start()
    tiles(0, HD, dn_part)
    dn_free.start()

    for dx in range(1, 4):
        x_peer(cx_s, cx_r, cx_send, cx_recv, dx).wait_recv()
    c_row = cx_r[0] + cx_r[1] + cx_r[2] + cx_r[3]
    c_s[0] = c_row
    c_r[0] = c_row
    spread(1, c_s, c_r, 2)

    far_up.wait_recv()

    def up_sum(cols):
        rs_up[:, cols] = (passage_part(1, cols) + rr_a[:, cols].astype(F32)).astype(BF16)

    tiles(0, HD, up_sum)
    up_last.start()
    far_dn.wait_recv()

    def dn_sum(cols):
        rs_dn[:, cols] = (passage_part(3, cols) + rr_a[:, cols].astype(F32)).astype(BF16)

    tiles(HD, HD, dn_sum)
    dn_last.start()

    h = jnp.zeros((ROWS, S), F32)
    for k in range(3):
        h = h + jnp.where(mask[k], hard_coef[k], 0.0)
    hmat[...] = h.astype(BF16)
    pair(gx_s, gx_r, 2).wait_recv()

    def query_grad(cols):
        part = mm(coef_o[...], PZ[:, cols]) + mm(hmat[...], RP[:, cols])
        gq_ref[:, cols] = part * LOGIT_SCALE + gx_r[:, cols].astype(F32)

    tiles(0, D, query_grad)

    spread_all(j_r, 1).wait_recv()
    spread_all(c_r, 2).wait_recv()
    j_row = fold(j_r).astype(jnp.int32)
    hmat[...] = jnp.where(iota((ROWS, S), 0) == j_row, fold(c_r), 0.0).astype(BF16)
    for ch in range(NCH):
        hard_all(1, ch).wait_recv()

        def passage_grad(cols):
            gp_ref[:, cols] = passage_part(0, cols) + LOGIT_SCALE * mm(hmat[...], RQ[:, cols])

        tiles(ch * DC, DC, passage_grad)
    up_free.wait_recv()
    dn_free.wait_recv()
    up_last.wait_recv()
    dn_last.wait_recv()

    def last(cols):
        gp_ref[:, cols] += rr_up[:, cols].astype(F32) + rr_dn[:, cols].astype(F32)

    tiles(0, D, last)

    for ch in range(NCH):
        for which in (0, 1):
            for kind in range(4):
                ring(which, kind, ch).wait_send()
            hard_all(which, ch).wait_send()
    for dx in range(1, 4):
        x_peer(xt_s, xt_r, xt_send, xt_recv, dx).wait_send()
        x_peer(cx_s, cx_r, cx_send, cx_recv, dx).wait_send()
    spread_all(w_r, 0).wait_send()
    spread_all(j_r, 1).wait_send()
    spread_all(c_r, 2).wait_send()
    pair(st_s, st_r, 0).wait_send()
    pair(lse_s, lse_r, 1).wait_send()
    pair(gx_s, gx_r, 2).wait_send()
    for copy in (far_up, far_dn, up_free, dn_free, up_last, dn_last):
        copy.wait_send()


def on_device(ngrp, queries, passages, positives, hard_owner, hard_row):
    D = queries.shape[1]
    NC = 2 if ngrp % 4 == 0 else 1
    NY = ngrp // (2 * NC)
    R = 4 * NY * NC
    S = 16 * R
    shift = math.log(8 * ROWS / 3)
    vmem = pltpu.VMEM
    dma = pltpu.SemaphoreType.DMA
    wide = vmem((ROWS, D), BF16)
    any_spec = pl.BlockSpec(memory_space=pl.ANY)
    vmem_spec = pl.BlockSpec(memory_space=pltpu.VMEM)
    loss, gq, gp = pl.pallas_call(
        functools.partial(kernel, NY, NC, D, shift),
        out_shape=(
            jax.ShapeDtypeStruct((1, ROWS), F32),
            jax.ShapeDtypeStruct((ROWS, D), F32),
            jax.ShapeDtypeStruct((ROWS, D), F32),
        ),
        in_specs=[any_spec, any_spec, vmem_spec, vmem_spec, vmem_spec],
        out_specs=(vmem_spec,) * 3,
        scratch_shapes=[
            vmem((4 * ROWS, D), BF16), vmem((4 * ROWS, D), BF16),
            vmem((S, D), BF16), vmem((S, D), BF16), vmem((S, D), BF16), vmem((S, D), BF16),
            wide, wide, wide, wide, wide, wide, wide, wide,
            vmem((ROWS, 4 * ROWS), F32), vmem((ROWS, 4 * ROWS), F32), vmem((ROWS, S), F32),
            vmem((2, S, 4 * ROWS), BF16),
            vmem((ROWS, 4 * ROWS), BF16), vmem((ROWS, 4 * ROWS), BF16), vmem((4 * ROWS, 2 * ROWS), BF16),
            vmem((ROWS, S), BF16),
            vmem((4, 8, S), F32), vmem((4, 8, S), F32),
            vmem((1, 1, S), F32), vmem((R, 1, S), F32),
            vmem((1, 1, S), F32), vmem((R, 1, S), F32),
            vmem((4, 1, S), F32), vmem((4, 1, S), F32),
            vmem((1, 1, S), F32), vmem((R, 1, S), F32),
            vmem((ROWS, 128), F32), vmem((ROWS, 128), F32), vmem((ROWS, 128), F32), vmem((ROWS, 128), F32),
            dma((2,)), dma((2, 4, NCH)), dma((2, 4, NCH)), dma((2, NCH)), dma((2, NCH)),
            dma((4,)), dma((4,)), dma((4,)), dma((4,)), dma((3,)), dma((3,)), dma((3,)), dma((3,)),
            dma((6,)), dma((6,)),
        ],
        compiler_params=pltpu.CompilerParams(
            collective_id=0, has_side_effects=True, vmem_limit_bytes=60 * 2**20
        ),
        cost_estimate=pl.CostEstimate(flops=9 * 10**9, bytes_accessed=8 * 2**20, transcendentals=2 * 10**5),
        name="infonce",
    )(queries, passages, positives, hard_owner, hard_row)
    return loss.reshape(ROWS), gq, gp


def solution(mesh):
    return jax.shard_map(
        functools.partial(on_device, mesh.shape["grp"]),
        mesh=mesh,
        in_specs=(
            P(("grp", "blk"), None),
            P(("grp", "blk"), None),
            P("grp", "blk"),
            P(("grp", "blk"), None),
            P(("grp", "blk"), None),
        ),
        out_specs=(P(("grp", "blk")), P(("grp", "blk"), None), P(("grp", "blk"), None)),
        check_vma=False,
    )
```

time: 370 us -> 176 us (0.48)
  waiting for transfers between devices: 193 us -> 0 us
  Pallas kernels: 0 us -> 166 us
  local copies, waits for them, and re-layouts: 68.6 us -> 8.6 us
  matrix products: 35.4 us -> 0 us
  blocking collectives: 21.4 us -> 0 us
  starting transfers between devices: 18.9 us -> 0 us
  other arithmetic: 16.4 us -> 0 us
  between operations: 14.2 us -> 0.64 us
    pallas_call x0 -> x1, Pallas kernels: none -> 166 us  [on_device(): pl.pallas_call(functools.partial(kernel, NY, NC, D, shift), out_shape=(ja...]
    all_to_all x2 -> x0, waiting for transfers between devices: 130 us -> none  [the longest x1 93.2 us: on_device(): lax.all_to_all(served, ('grp', 'blk'), split_axis=0, concat_axis=0, tiled...]
    reduce_scatter x1 -> x0, waiting for transfers between devices: 62.3 us -> none  [on_device(): lax.psum_scatter((jnp.einsum('qj,qd->jd', coef, queries, preferred_elemen...]
    dot_general x6 -> x0, matrix products: 35.4 us -> none  [the longest x1 8.09 us: on_device(): jnp.einsum('qd,qkd->qk', queries, hard, preferred_element_type=jnp.float32)]
    reshape x7 -> x0, local copies, waits for them, and re-layouts: 33.2 us -> none  [the longest x2 11.3 us: on_device(): hard = fetched.reshape(-1, width)[slot].reshape(rows, nhard, width)]
    all_to_all x1 -> x0, blocking collectives: 21.4 us -> none  [on_device(): lax.all_to_all(wanted, ('grp', 'blk'), split_axis=0, concat_axis=0, tiled...]
    all_to_all x2 -> x0, starting transfers between devices: 18.8 us -> none  [the longest x1 11.9 us: on_device(): lax.all_to_all(served, ('grp', 'blk'), split_axis=0, concat_axis=0, tiled...]
    mul x5 -> x0, local copies, waits for them, and re-layouts: 15.1 us -> none  [the longest x3 14.8 us: on_device(): LOGIT_SCALE * hard_coef[:, :, None]]
  transfers between devices with their start and end apart: 4 -> 0, of which waited for: 3 -> 0; matrix products, arithmetic and copies ran while one was open for 28% -> 0% of each run, Pallas kernels for 0% -> 0%
where the time goes in v1:
time: 176 us
  Pallas kernels  166 us (94%)
  local copies, waits for them, and re-layouts  8.6 us (5%)
    pallas_call x1, Pallas kernels, on_device(): pl.pallas_call(functools.partial(kernel, NY, NC, D, shift), out_shape=(ja...  166 us
    unnamed x7, local copies, waits for them, and re-layouts  8.6 us

profile of v1, /device:TPU:1, one launch (start us, length us, event | category | flops | bytes accessed | tf_op | source)
XLA Modules:
  0.0 175.5 jit_solution(8455902049615877870)
XLA Ops:
  0.6 1.4 copy.8.own_ref
  2.0 1.4 copy.9.row_ref
  3.5 166.3 %infonce.1 = (f32[1,128]{1,0:T(1,128)}, f32[128,4096]{1,0:T(8,128)}, f32[128,4096]{1,0:T(8,128)}) custom-call(bf16[128,4096]{1,0:T(8,128)(2,1)} %q_hbm.1, bf16[128,4096]{1,0:T(8,128)(2,1)} %p_hbm.1, s32[1,128]{1,0:T(1,128)} %pos_ref.1, s32[128,3]{1,0:T(8,128)} %copy.8.own_ref, s32[128,3]{1,0:T(8,128)} %copy.9.row_ref), custom_call_target="tpu_custom_call" | custom-call | flops 8999999488 | bytes 8388608 | tf_op jit(solution)/shard_map/infonce/pallas_call | solution.py:520
  169.8 1.2 copy.13
  171.0 0.0 copy-start
  171.0 3.3 %copy.14 = f32[128,4096]{1,0:T(8,128)} copy(f32[128,4096]{1,0:T(8,128)} %get-tuple-element.13) | data formatting | bytes 4194304
  174.2 0.0 copy-done
  174.2 1.3 copy.15
Async XLA Ops:
  171.0 3.3 %copy-start = (f32[128,4096]{1,0:T(8,128)S(1)}, f32[128,4096]{1,0:T(8,128)}, u32[]{:S(2)}) copy-start(f32[128,4096]{1,0:T(8,128)} %get-tuple-element.14) | copy-start | bytes 6291460

commit v2 on v1

--- a/solution.py
+++ b/solution.py
@@ -45,12 +45,12 @@
 def kernel(
     NY, NC, D, shift,
     q_hbm, p_hbm, pos_ref, own_ref, row_ref,
-    loss_ref, gq_ref, gp_ref,
+    loss_ref, gq_hbm, gp_hbm,
     PZ, QX, SP, SQ, RP, RQ,
     rs_a, rs_up, rs_dn, rr_a, rr_up, rr_dn, gx_s, gx_r,
     s_own, s_par, hs, gather, coef_o, coef_p, coef_t, hmat,
-    xt_s, xt_r, w_s, w_r, j_s, j_r, cx_s, cx_r, c_s, c_r, st_s, st_r, lse_s, lse_r,
-    in_sem, ag_send, ag_recv, hard_send, hard_recv,
+    xt_s, xt_r, w_s, w_r, cx_s, cx_r, c_s, c_r, st_s, st_r, lse_s, lse_r, gq_ref, gp_ref,
+    in_sem, out_sem, ag_send, ag_recv, hard_send, hard_recv,
     xt_send, xt_recv, cx_send, cx_recv, small_send, small_recv, pair_send, pair_recv, rs_send, rs_recv,
 ):
     R = 4 * NY * NC
@@ -102,6 +102,54 @@
         return carry
 
     lax.fori_loop(0, R, greet, 0)
+    lane = iota((1, S), 1)
+    slot_r = lane // 16
+    slot_b = lax.rem(lane, 16) // 4
+    slot_t = lax.rem(lane, 4)
+    r_a = slot_r // (NY * NC)
+    r_y = lax.rem(slot_r // NC, NY)
+    r_c = lax.rem(slot_r, NC)
+
+    def dev_id(x2, y2, z2, c2):
+        return ((y2 * 2 + lax.rem(x2, 2)) * NC + c2) * 8 + (x2 // 2) * 4 + z2
+
+    owner = [to_column(own_ref[k : k + 1, :].astype(F32)) for k in range(3)]
+    hrow = [to_column(row_ref[k : k + 1, :].astype(F32)) for k in range(3)]
+    ndev = 8 * 2 * NY * NC
+    lane_o = iota((ROWS, max(ndev, 128)), 1).astype(F32)
+    hot = [(owner[k] == lane_o).astype(F32) for k in range(3)]
+    count = hot[0] + hot[1] + hot[2]
+    lower = (iota((ROWS, ROWS), 1) < iota((ROWS, ROWS), 0)).astype(BF16)
+    before = mm(lower, count.astype(BF16))
+    rank = [jnp.sum(h * before, axis=1, keepdims=True) for h in hot]
+    codes = [jnp.where(owner[k] >= 0, owner[k] * CAP + rank[k], -1.0) for k in range(3)]
+    codes_p = (
+        dev_id(lax.rem(x + 4 - r_a, 4), lax.rem(y + NY - r_y, NY), slot_b, lax.rem(c + NC - r_c, NC)) * CAP + slot_t
+    ).astype(F32)
+
+    def codes_q(dx):
+        full = dev_id(lax.rem(x + dx, 4), lax.rem(y + r_y, NY), lax.rem(z + r_a, 4), lax.rem(c + r_c, NC)) * CAP + slot_t
+        return jnp.where(slot_b == x, full, -2).astype(F32)
+
+    def pick(code_row, values):
+        total = jnp.zeros((ROWS, S), F32)
+        for k in range(3):
+            total = total + jnp.where(codes[k] == code_row, values[k], 0.0)
+        return jnp.sum(total, axis=0, keepdims=True)
+
+    w_row = pick(codes_p, hrow)
+    w_s[0] = w_row
+    w_r[0] = w_row
+    query_number = iota((ROWS, 1), 0).astype(F32)
+    query_and_row = [query_number + ROWS * hrow[k] for k in range(3)]
+    pos_row = pos_ref[...].astype(F32)
+    pos_wide = jnp.concatenate([pos_row] + [jnp.zeros((1, S - ROWS), F32)], axis=1)
+    for dx in range(4):
+        table = jnp.where(iota((2, S), 0) == 0, pick(codes_q(dx), query_and_row), pos_wide)
+        xt_s[dx] = table
+        if dx == 0:
+            xt_r[0] = table
+
     pl.semaphore_wait(barrier, (R - 1) + 3 * NY * NC)
     p_in.wait()
     q_in.wait()
@@ -138,54 +186,6 @@
             ring(which, 0, ch).start()
             ring(which, 1, ch).start()
 
-    own_sends(0)
-    own_sends(1)
-
-    lane = iota((1, S), 1)
-    slot_r = lane // 16
-    slot_b = lax.rem(lane, 16) // 4
-    slot_t = lax.rem(lane, 4)
-    r_a = slot_r // (NY * NC)
-    r_y = lax.rem(slot_r // NC, NY)
-    r_c = lax.rem(slot_r, NC)
-
-    def dev_id(x2, y2, z2, c2):
-        return ((y2 * 2 + lax.rem(x2, 2)) * NC + c2) * 8 + (x2 // 2) * 4 + z2
-
-    owner = own_ref[...]
-    hrow = row_ref[...].astype(F32)
-    ndev = 8 * 2 * NY * NC
-    width = max(ndev, 128)
-    lane_o = iota((ROWS, width), 1)
-    hot = [(owner[:, k : k + 1] == lane_o).astype(F32) for k in range(3)]
-    count = hot[0] + hot[1] + hot[2]
-    lower = (iota((ROWS, ROWS), 1) < iota((ROWS, ROWS), 0)).astype(BF16)
-    before = mm(lower, count.astype(BF16))
-    rank = [jnp.sum(h * before, axis=1, keepdims=True).astype(jnp.int32) for h in hot]
-
-    def code(k):
-        return owner[:, k : k + 1] * CAP + rank[k]
-
-    codes = [jnp.where(owner[:, k : k + 1] >= 0, code(k), -1) for k in range(3)]
-    codes_p = (
-        dev_id(lax.rem(x + 4 - r_a, 4), lax.rem(y + NY - r_y, NY), slot_b, lax.rem(c + NC - r_c, NC)) * CAP + slot_t
-    )
-
-    def codes_q(dx):
-        full = dev_id(lax.rem(x + dx, 4), lax.rem(y + r_y, NY), lax.rem(z + r_a, 4), lax.rem(c + r_c, NC)) * CAP + slot_t
-        return jnp.where(slot_b == x, full, -2)
-
-    def pick(code_row, values):
-        total = jnp.zeros((ROWS, S), F32)
-        for k in range(3):
-            total = total + jnp.where(codes[k] == code_row, values[k], 0.0)
-        return jnp.sum(total, axis=0, keepdims=True)
-
-    rows_k = [hrow[:, k : k + 1] for k in range(3)]
-    w_row = pick(codes_p, rows_k)
-    w_s[0] = w_row
-    w_r[0] = w_row
-
     def spread(kind, src, dst, wide):
         def body(n, carry):
             a, yy, cc, r = order(n)
@@ -211,47 +211,18 @@
 
     def fold(ref):
         values = ref[...]
-        keep = iota((R, 1, S), 2) // 16 == iota((R, 1, S), 0)
+        keep = iota(values.shape, 2) // 16 == iota(values.shape, 0)
         return jnp.sum(jnp.where(keep, values, 0.0), axis=0)
 
-    spread(0, w_s, w_r, 0)
-
-    query_number = iota((ROWS, 1), 0).astype(F32)
-    pos_row = pos_ref[...].astype(F32)
-    pos_wide = jnp.concatenate([pos_row] + [jnp.zeros((1, S - ROWS), F32)], axis=1)
-    sub8 = iota((8, S), 0)
-    for dx in range(4):
-        cq = codes_q(dx)
-        v_row = pick(cq, [query_number] * 3)
-        jj_row = pick(cq, rows_k)
-        table = jnp.where(sub8 == 0, v_row, 0.0) + jnp.where(sub8 == 1, jj_row, 0.0) + jnp.where(sub8 == 2, pos_wide, 0.0)
-        xt_s[dx] = table
-        if dx == 0:
-            xt_r[0] = table
-
     def x_peer(src, dst, send, recv, dx):
         return pltpu.make_async_remote_copy(
             src.at[dx], dst.at[dx], send.at[dx], recv.at[dx], device_id=dev(dx, 0, 0, 0), device_id_type=MESH
         )
-
-    for dx in range(1, 4):
-        x_peer(xt_s, xt_r, xt_send, xt_recv, dx).start()
-    for dx in range(1, 4):
-        x_peer(xt_s, xt_r, xt_send, xt_recv, dx).wait_recv()
-    tables = xt_r[0] + xt_r[1] + xt_r[2] + xt_r[3]
-    v_all = tables[0:1, :]
-    j_s[0] = tables[1:2, :]
-    j_r[0] = tables[1:2, :]
-    spread(1, j_s, j_r, 1)
 
     def gather_matrix(index, slot):
         n = iota((S, 1), 0)
         want = to_column(index).astype(jnp.int32) + lax.rem(n, 16) // 4 * ROWS
         gather[slot] = (want == iota((S, 4 * ROWS), 1)).astype(BF16)
-
-    spread_all(w_r, 0).wait_recv()
-    gather_matrix(fold(w_r), 0)
-    gather_matrix(v_all, 1)
 
     def hard_starts(kind, ch):
         src, dst = ((SP, RP), (SQ, RQ))[kind]
@@ -308,30 +279,44 @@
 
         tiles(ch * DC, DC, body)
 
-    for ch in range(NCH):
+    def forward(ch):
         for which in (0, 1):
             for kind in (0, 1):
                 arriving(which, kind, ch).wait_recv()
                 ring(which, kind + 2, ch).start()
-        if ch + 2 < NCH:
-            own_sends(ch + 2)
-        arriving(0, 2, ch).wait_recv()
-        arriving(0, 3, ch).wait_recv()
-        serve(0, ch)
-        hard_starts(0, ch)
+
+    own_sends(0)
+    spread(0, w_s, w_r, 0)
+    for dx in range(1, 4):
+        x_peer(xt_s, xt_r, xt_send, xt_recv, dx).start()
+    own_sends(1)
+    spread_all(w_r, 0).wait_recv()
+    gather_matrix(fold(w_r), 0)
+    forward(0)
+    own_sends(2)
+    for dx in range(1, 4):
+        x_peer(xt_s, xt_r, xt_send, xt_recv, dx).wait_recv()
+    tables = (xt_r[0] + xt_r[1] + xt_r[2] + xt_r[3])[0:1, :].astype(jnp.int32)
+    j_all = (tables // ROWS).astype(F32)
+    gather_matrix(lax.rem(tables, ROWS).astype(F32), 1)
+
+    for ch in range(NCH):
+        if ch + 1 < NCH:
+            forward(ch + 1)
+        if ch + 3 < NCH:
+            own_sends(ch + 3)
+        for kind in (0, 1):
+            arriving(kind, 2, ch).wait_recv()
+            arriving(kind, 3, ch).wait_recv()
+            serve(kind, ch)
+            hard_starts(kind, ch)
         score(s_own, me_rows, PZ, ch)
-    for ch in range(NCH):
-        arriving(1, 2, ch).wait_recv()
-        arriving(1, 3, ch).wait_recv()
-        serve(1, ch)
-        hard_starts(1, ch)
-    for ch in range(NCH):
         score(s_par, par_rows, PZ, ch)
 
     base = (xh * 4 * ROWS).astype(F32)
     lane_p = iota((ROWS, 4 * ROWS), 1).astype(F32)
     pos_own = to_column(pos_row) - base
-    pos_par = to_column(xt_r[2][2:3, 0:ROWS]) - base
+    pos_par = to_column(xt_r[2][1:2, 0:ROWS]) - base
 
     def half_stats(acc, pos):
         s = acc[...] * LOGIT_SCALE
@@ -361,7 +346,7 @@
     scaled = hs[...] * LOGIT_SCALE + shift
     mask = [codes[k] == codes_p for k in range(3)]
     hard_k = [jnp.sum(jnp.where(mask[k], scaled, 0.0), axis=1, keepdims=True) for k in range(3)]
-    present = [jnp.where(owner[:, k : k + 1] >= 0, hard_k[k], NEG) for k in range(3)]
+    present = [jnp.where(owner[k] >= 0, hard_k[k], NEG) for k in range(3)]
     top = jnp.maximum(jnp.maximum(m_o, m_r), jnp.maximum(jnp.maximum(present[0], present[1]), present[2]))
     total = l_o * jnp.exp(m_o - top) + l_r * jnp.exp(m_r - top)
     for k in range(3):
@@ -435,9 +420,10 @@
     for dx in range(1, 4):
         x_peer(cx_s, cx_r, cx_send, cx_recv, dx).wait_recv()
     c_row = cx_r[0] + cx_r[1] + cx_r[2] + cx_r[3]
-    c_s[0] = c_row
-    c_r[0] = c_row
-    spread(1, c_s, c_r, 2)
+    both = jnp.where(iota((2, S), 0) == 0, c_row, j_all)
+    c_s[0] = both
+    c_r[0] = both
+    spread(1, c_s, c_r, 1)
 
     far_up.wait_recv()
 
@@ -465,11 +451,12 @@
         gq_ref[:, cols] = part * LOGIT_SCALE + gx_r[:, cols].astype(F32)
 
     tiles(0, D, query_grad)
-
-    spread_all(j_r, 1).wait_recv()
-    spread_all(c_r, 2).wait_recv()
-    j_row = fold(j_r).astype(jnp.int32)
-    hmat[...] = jnp.where(iota((ROWS, S), 0) == j_row, fold(c_r), 0.0).astype(BF16)
+    gq_out = pltpu.make_async_copy(gq_ref, gq_hbm, out_sem.at[0])
+    gq_out.start()
+
+    spread_all(c_r, 1).wait_recv()
+    both = fold(c_r)
+    hmat[...] = jnp.where(query_number == both[1:2, :], both[0:1, :], 0.0).astype(BF16)
     for ch in range(NCH):
         hard_all(1, ch).wait_recv()
 
@@ -485,7 +472,12 @@
     def last(cols):
         gp_ref[:, cols] += rr_up[:, cols].astype(F32) + rr_dn[:, cols].astype(F32)
 
-    tiles(0, D, last)
+    outs = [gq_out]
+    for ch in range(4):
+        tiles(ch * D // 4, D // 4, last)
+        cols = pl.ds(ch * D // 4, D // 4)
+        outs.append(pltpu.make_async_copy(gp_ref.at[:, cols], gp_hbm.at[:, cols], out_sem.at[1 + ch]))
+        outs[-1].start()
 
     for ch in range(NCH):
         for which in (0, 1):
@@ -496,13 +488,20 @@
         x_peer(xt_s, xt_r, xt_send, xt_recv, dx).wait_send()
         x_peer(cx_s, cx_r, cx_send, cx_recv, dx).wait_send()
     spread_all(w_r, 0).wait_send()
-    spread_all(j_r, 1).wait_send()
-    spread_all(c_r, 2).wait_send()
+    spread_all(c_r, 1).wait_send()
     pair(st_s, st_r, 0).wait_send()
     pair(lse_s, lse_r, 1).wait_send()
     pair(gx_s, gx_r, 2).wait_send()
     for copy in (far_up, far_dn, up_free, dn_free, up_last, dn_last):
         copy.wait_send()
+    for copy in outs:
+        copy.wait()
+
+
+def results(loss_in, gq_in, gp_in, loss_out, gq_out, gp_out):
+    loss_out[...] = loss_in[...]
+    gq_out[...] = gq_in[...]
+    gp_out[...] = gp_in[...]
 
 
 def on_device(ngrp, queries, passages, positives, hard_owner, hard_row):
@@ -525,7 +524,7 @@
             jax.ShapeDtypeStruct((ROWS, D), F32),
         ),
         in_specs=[any_spec, any_spec, vmem_spec, vmem_spec, vmem_spec],
-        out_specs=(vmem_spec,) * 3,
+        out_specs=(vmem_spec, any_spec, any_spec),
         scratch_shapes=[
             vmem((4 * ROWS, D), BF16), vmem((4 * ROWS, D), BF16),
             vmem((S, D), BF16), vmem((S, D), BF16), vmem((S, D), BF16), vmem((S, D), BF16),
@@ -534,14 +533,14 @@
             vmem((2, S, 4 * ROWS), BF16),
             vmem((ROWS, 4 * ROWS), BF16), vmem((ROWS, 4 * ROWS), BF16), vmem((4 * ROWS, 2 * ROWS), BF16),
             vmem((ROWS, S), BF16),
-            vmem((4, 8, S), F32), vmem((4, 8, S), F32),
-            vmem((1, 1, S), F32), vmem((R, 1, S), F32),
+            vmem((4, 2, S), F32), vmem((4, 2, S), F32),
             vmem((1, 1, S), F32), vmem((R, 1, S), F32),
             vmem((4, 1, S), F32), vmem((4, 1, S), F32),
-            vmem((1, 1, S), F32), vmem((R, 1, S), F32),
+            vmem((1, 2, S), F32), vmem((R, 2, S), F32),
             vmem((ROWS, 128), F32), vmem((ROWS, 128), F32), vmem((ROWS, 128), F32), vmem((ROWS, 128), F32),
-            dma((2,)), dma((2, 4, NCH)), dma((2, 4, NCH)), dma((2, NCH)), dma((2, NCH)),
-            dma((4,)), dma((4,)), dma((4,)), dma((4,)), dma((3,)), dma((3,)), dma((3,)), dma((3,)),
+            vmem((ROWS, D), F32), vmem((ROWS, D), F32),
+            dma((2,)), dma((5,)), dma((2, 4, NCH)), dma((2, 4, NCH)), dma((2, NCH)), dma((2, NCH)),
+            dma((4,)), dma((4,)), dma((4,)), dma((4,)), dma((2,)), dma((2,)), dma((3,)), dma((3,)),
             dma((6,)), dma((6,)),
         ],
         compiler_params=pltpu.CompilerParams(
@@ -549,7 +548,17 @@
         ),
         cost_estimate=pl.CostEstimate(flops=9 * 10**9, bytes_accessed=8 * 2**20, transcendentals=2 * 10**5),
         name="infonce",
-    )(queries, passages, positives, hard_owner, hard_row)
+    )(queries, passages, positives, hard_owner.T, hard_row.T)
+    block = pl.BlockSpec((ROWS // 4, D), lambda i: (i, 0))
+    row = pl.BlockSpec((1, ROWS), lambda i: (0, 0))
+    loss, gq, gp = pl.pallas_call(
+        results,
+        grid=(4,),
+        in_specs=[row, block, block],
+        out_specs=(row, block, block),
+        out_shape=tuple(jax.ShapeDtypeStruct(a.shape, F32) for a in (loss, gq, gp)),
+        name="results",
+    )(loss, gq, gp)
     return loss.reshape(ROWS), gq, gp
 
 

time: 176 us -> 166 us (0.943)
  local copies, waits for them, and re-layouts: 8.6 us -> 0 us
    unnamed x7 -> x0, local copies, waits for them, and re-layouts: 8.6 us -> none
    pallas_call x1, Pallas kernels: 166 us -> 160 us  [on_device(): pl.pallas_call(functools.partial(kernel, NY, NC, D, shift), out_shape=(ja...]
    pallas_call x0 -> x1, Pallas kernels: none -> 4.7 us  [on_device(): pl.pallas_call(results, grid=(4,), in_specs=[row, block, block], out_spec...]
where the time goes in v2:
time: 166 us; the launch traced here: 165 us
  Pallas kernels  165 us (99%)
    pallas_call x1, Pallas kernels, on_device(): pl.pallas_call(functools.partial(kernel, NY, NC, D, shift), out_shape=(ja...  160 us
    pallas_call x1, Pallas kernels, on_device(): pl.pallas_call(results, grid=(4,), in_specs=[row, block, block], out_spec...  4.7 us

profile of v2, /device:TPU:1, one launch (start us, length us, event | category | flops | bytes accessed | tf_op | source)
XLA Modules:
  0.0 165.5 jit_solution(10512230508764687988)
XLA Ops:
  0.6 160.1 %infonce.1 = (f32[1,128]{1,0:T(1,128)}, f32[128,4096]{1,0:T(8,128)}, f32[128,4096]{1,0:T(8,128)}) custom-call(bf16[128,4096]{1,0:T(8,128)(2,1)} %q_hbm.1, bf16[128,4096]{1,0:T(8,128)(2,1)} %p_hbm.1, s32[1,128]{1,0:T(1,128)} %pos_ref.1, s32[3,128]{1,0:T(4,128)} %bitcast.3, s32[3,128]{1,0:T(4,128)} %bitcast.4), custom_call_target="tpu_custom_call" | custom-call | flops 8999999488 | bytes 8388608 | tf_op jit(solution)/shard_map/infonce/pallas_call | solution.py:519
  160.8 4.7 %results.1 = (f32[1,128]{1,0:T(1,128)}, f32[128,4096]{1,0:T(8,128)}, f32[128,4096]{1,0:T(8,128)}) custom-call(f32[1,128]{1,0:T(1,128)} %get-tuple-element.9.loss_in, f32[128,4096]{1,0:T(8,128)} %get-tuple-element.10.gq_in, f32[128,4096]{1,0:T(8,128)} %get-tuple-element.11.gp_in), custom_call_target="tpu_custom_call" | custom-call | tf_op jit(solution)/shard_map/results/pallas_call | solution.py:554

commit v3 on v2

--- a/solution.py
+++ b/solution.py
@@ -12,6 +12,7 @@
 ROWS = 128
 CAP = 4
 NCH = 4
+EARLY = (1, 2)
 NEG = -1e30
 MESH = pl.DeviceIdType.MESH
 F32 = jnp.float32
@@ -46,15 +47,17 @@
     NY, NC, D, shift,
     q_hbm, p_hbm, pos_ref, own_ref, row_ref,
     loss_ref, gq_hbm, gp_hbm,
-    PZ, QX, SP, SQ, RP, RQ,
+    PZ, QX, SP, SQ, RP, MQ, RQ,
     rs_a, rs_up, rs_dn, rr_a, rr_up, rr_dn, gx_s, gx_r,
     s_own, s_par, hs, gather, coef_o, coef_p, coef_t, hmat,
-    xt_s, xt_r, w_s, w_r, cx_s, cx_r, c_s, c_r, st_s, st_r, lse_s, lse_r, gq_ref, gp_ref,
+    xt_s, xt_r, w_s, w_r, cx_s, cx_r, cz_s, cz_r, c_s, c_r, st_s, st_r, lse_s, lse_r, gq_ref, gp_ref,
     in_sem, out_sem, ag_send, ag_recv, hard_send, hard_recv,
-    xt_send, xt_recv, cx_send, cx_recv, small_send, small_recv, pair_send, pair_recv, rs_send, rs_recv,
+    xt_send, xt_recv, cx_send, cx_recv, cz_send, cz_recv, turn_send, turn_recv, small_send, small_recv, pair_send, pair_recv, rs_send, rs_recv,
 ):
     R = 4 * NY * NC
     S = 16 * R
+    HR = S // 4
+    SECOND = [0] + sorted(range(1, NY * NC), key=lambda m: (m % NC, m // NC == 2, m))
     DC = D // NCH
     H = DC // 2
     HD = D // 2
@@ -95,13 +98,11 @@
         def _():
             pl.semaphore_signal(barrier, inc=1, device_id=dev(a, yy, 0, cc), device_id_type=MESH)
 
-        @pl.when(a > 0)
-        def _():
-            pl.semaphore_signal(barrier, inc=1, device_id=dev(0, yy, a, cc), device_id_type=MESH)
-
         return carry
 
     lax.fori_loop(0, R, greet, 0)
+    for dz in range(1, 4):
+        pl.semaphore_signal(barrier, inc=1, device_id=dev(0, 0, dz, 0), device_id_type=MESH)
     lane = iota((1, S), 1)
     slot_r = lane // 16
     slot_b = lax.rem(lane, 16) // 4
@@ -150,7 +151,7 @@
         if dx == 0:
             xt_r[0] = table
 
-    pl.semaphore_wait(barrier, (R - 1) + 3 * NY * NC)
+    pl.semaphore_wait(barrier, R - 1 + 3)
     p_in.wait()
     q_in.wait()
 
@@ -186,33 +187,49 @@
             ring(which, 0, ch).start()
             ring(which, 1, ch).start()
 
-    def spread(kind, src, dst, wide):
-        def body(n, carry):
-            a, yy, cc, r = order(n)
-
-            @pl.when(r > 0)
-            def _():
-                neg = (lax.rem(4 - a, 4), lax.rem(NY - yy, NY), lax.rem(NC - cc, NC))
-                target = dev(neg[0], neg[1], 0, neg[2]) if kind == 0 else dev(0, yy, a, cc)
-                pltpu.make_async_remote_copy(
-                    src.at[0], dst.at[r], small_send.at[wide], small_recv.at[wide],
-                    device_id=target, device_id_type=MESH,
-                ).start()
-
-            return carry
-
-        lax.fori_loop(0, R, body, 0)
-
-    def spread_all(dst, wide):
-        return pltpu.make_async_remote_copy(
-            dst.at[pl.ds(1, R - 1)], dst.at[pl.ds(1, R - 1)], small_send.at[wide], small_recv.at[wide],
-            device_id=dev(1, 0, 0, 0), device_id_type=MESH,
-        )
-
-    def fold(ref):
+    def ask(n, carry):
+        a, yy, cc, r = order(n)
+
+        @pl.when(r > 0)
+        def _():
+            target = dev(lax.rem(4 - a, 4), lax.rem(NY - yy, NY), 0, lax.rem(NC - cc, NC))
+            pltpu.make_async_remote_copy(
+                w_s.at[0], w_r.at[r], small_send.at[0], small_recv.at[0], device_id=target, device_id_type=MESH
+            ).start()
+
+        return carry
+
+    def asked():
+        ref = w_r.at[pl.ds(1, R - 1)]
+        return pltpu.make_async_remote_copy(
+            ref, ref, small_send.at[0], small_recv.at[0], device_id=dev(1, 0, 0, 0), device_id_type=MESH
+        )
+
+    def z_peer(dz):
+        return pltpu.make_async_remote_copy(
+            cz_s.at[0], cz_r.at[dz], cz_send.at[dz], cz_recv.at[dz], device_id=dev(0, 0, dz, 0), device_id_type=MESH
+        )
+
+    def yc_peer(m):
+        return pltpu.make_async_remote_copy(
+            c_s.at[0], c_r.at[m], small_send.at[1], small_recv.at[1],
+            device_id=dev(0, m // NC, 0, m % NC), device_id_type=MESH,
+        )
+
+    def yc_all():
+        ref = c_r.at[pl.ds(1, NY * NC - 1)]
+        return pltpu.make_async_remote_copy(
+            ref, ref, small_send.at[1], small_recv.at[1], device_id=dev(1, 0, 0, 0), device_id_type=MESH
+        )
+
+    def fold(ref, group):
         values = ref[...]
-        keep = iota(values.shape, 2) // 16 == iota(values.shape, 0)
-        return jnp.sum(jnp.where(keep, values, 0.0), axis=0)
+        total = jnp.zeros(values.shape[1:], F32)
+        for n in range(values.shape[0]):
+            total = total + jnp.where(group == n, values[n], 0.0)
+        return total
+
+    slot_number = slot_r
 
     def x_peer(src, dst, send, recv, dx):
         return pltpu.make_async_remote_copy(
@@ -224,18 +241,15 @@
         want = to_column(index).astype(jnp.int32) + lax.rem(n, 16) // 4 * ROWS
         gather[slot] = (want == iota((S, 4 * ROWS), 1)).astype(BF16)
 
-    def hard_starts(kind, ch):
-        src, dst = ((SP, RP), (SQ, RQ))[kind]
-
+    def hard_starts(ch):
         def body(n, carry):
             a, yy, cc, r = order(n)
 
             @pl.when(r > 0)
             def _():
-                target = dev(a, yy, 0, cc) if kind == 0 else dev(0, yy, a, cc)
                 pltpu.make_async_remote_copy(
-                    src.at[pl.ds(r * 16, 16), pl.ds(ch * DC, DC)], dst.at[pl.ds(r * 16, 16), pl.ds(ch * DC, DC)],
-                    hard_send.at[kind, ch], hard_recv.at[kind, ch], device_id=target, device_id_type=MESH,
+                    SP.at[pl.ds(r * 16, 16), pl.ds(ch * DC, DC)], RP.at[pl.ds(r * 16, 16), pl.ds(ch * DC, DC)],
+                    hard_send.at[0, ch], hard_recv.at[0, ch], device_id=dev(a, yy, 0, cc), device_id_type=MESH,
                 ).start()
 
             return carry
@@ -243,12 +257,30 @@
         lax.fori_loop(0, R, body, 0)
 
     def hard_all(kind, ch):
-        src, dst = ((SP, RP), (SQ, RQ))[kind]
-        ref = lambda buf: buf.at[pl.ds(16, S - 16), pl.ds(ch * DC, DC)]
-        return pltpu.make_async_remote_copy(
-            ref(src), ref(dst), hard_send.at[kind, ch], hard_recv.at[kind, ch],
-            device_id=dev(1, 0, 0, 0), device_id_type=MESH,
-        )
+        cols = pl.ds(ch * DC, DC)
+        ref = RP.at[pl.ds(16, S - 16), cols] if kind == 0 else RQ.at[:, pl.ds(16, HR - 16), cols]
+        return pltpu.make_async_remote_copy(
+            ref, ref, hard_send.at[kind, ch], hard_recv.at[kind, ch], device_id=dev(1, 0, 0, 0), device_id_type=MESH
+        )
+
+    def turn(dz, ch):
+        cols = pl.ds(ch * DC, DC)
+        return pltpu.make_async_remote_copy(
+            SQ.at[dz, :, cols], MQ.at[dz, :, cols], turn_send.at[dz, ch], turn_recv.at[dz, ch],
+            device_id=dev(0, 0, dz, 0), device_id_type=MESH,
+        )
+
+    def second(ch):
+        cols = pl.ds(ch * DC, DC)
+        for dz in range(1, 4):
+            turn(dz, ch).wait_recv()
+        for m in SECOND[1:]:
+            part = pl.ds(m * 16, 16)
+            pltpu.make_async_remote_copy(
+                MQ.at[:, part, cols], RQ.at[:, part, cols], hard_send.at[1, ch], hard_recv.at[1, ch],
+                device_id=dev(0, m // NC, 0, m % NC), device_id_type=MESH,
+            ).start()
+        RQ[:, 0:16, cols] = MQ[:, 0:16, cols]
 
     def tiles(start, length, body):
         def step(t, carry):
@@ -257,15 +289,15 @@
 
         lax.fori_loop(0, length // TN, step, 0)
 
-    def serve(kind, ch):
-        src, out, mine = ((PZ, SP, RP), (QX, SQ, RQ))[kind]
-
-        def body(cols):
-            rows = mm(gather[kind], src[:, cols]).astype(BF16)
-            out[:, cols] = rows
-            mine[0:16, cols] = rows[0:16]
-
-        tiles(ch * DC, DC, body)
+    def serve_p(cols):
+        rows = mm(gather[0], PZ[:, cols]).astype(BF16)
+        SP[:, cols] = rows
+        RP[0:16, cols] = rows[0:16]
+
+    def serve_q(cols):
+        rows = mm(gather[1], QX[:, cols]).astype(BF16)
+        for dz in range(4):
+            (MQ if dz == 0 else SQ)[dz, :, cols] = rows[dz * HR : (dz + 1) * HR]
 
     me_rows = pl.ds(x * ROWS, ROWS)
     par_rows = pl.ds(lax.rem(x + 2, 4) * ROWS, ROWS)
@@ -286,12 +318,12 @@
                 ring(which, kind + 2, ch).start()
 
     own_sends(0)
-    spread(0, w_s, w_r, 0)
+    lax.fori_loop(0, R, ask, 0)
     for dx in range(1, 4):
         x_peer(xt_s, xt_r, xt_send, xt_recv, dx).start()
     own_sends(1)
-    spread_all(w_r, 0).wait_recv()
-    gather_matrix(fold(w_r), 0)
+    asked().wait_recv()
+    gather_matrix(fold(w_r, slot_number), 0)
     forward(0)
     own_sends(2)
     for dx in range(1, 4):
@@ -305,11 +337,15 @@
             forward(ch + 1)
         if ch + 3 < NCH:
             own_sends(ch + 3)
-        for kind in (0, 1):
-            arriving(kind, 2, ch).wait_recv()
-            arriving(kind, 3, ch).wait_recv()
-            serve(kind, ch)
-            hard_starts(kind, ch)
+        arriving(0, 2, ch).wait_recv()
+        arriving(0, 3, ch).wait_recv()
+        tiles(ch * DC, DC, serve_p)
+        hard_starts(ch)
+        arriving(1, 2, ch).wait_recv()
+        arriving(1, 3, ch).wait_recv()
+        tiles(ch * DC, DC, serve_q)
+        for dz in (1, 3, 2):
+            turn(dz, ch).start()
         score(s_own, me_rows, PZ, ch)
         score(s_par, par_rows, PZ, ch)
 
@@ -340,6 +376,8 @@
     for ch in range(NCH):
         hard_all(0, ch).wait_recv()
         score(hs, me_rows, RP, ch)
+        if ch in EARLY:
+            second(EARLY.index(ch))
     pair(st_s, st_r, 0).wait_recv()
     stats = st_r[...]
     m_r, l_r, sp_r = stats[:, 0:1], stats[:, 1:2], stats[:, 2:3]
@@ -357,6 +395,41 @@
     loss_ref[...] = to_row(lse - (sp_o + sp_r))
     hard_coef = [jnp.exp(present[k] - lse) for k in range(3)]
 
+    def half_coef(acc, pos, row_lse, out, column):
+        f = jnp.exp(acc[...] * LOGIT_SCALE - row_lse) - jnp.where(lane_p == pos, 1.0, 0.0)
+        out[...] = f.astype(BF16)
+        coef_t[:, column * ROWS : (column + 1) * ROWS] = jnp.transpose(f).astype(BF16)
+
+    half_coef(s_own, pos_own, lse, coef_o, 0)
+    pair(lse_s, lse_r, 1).wait_recv()
+    half_coef(s_par, pos_par, lse_r[:, 0:1], coef_p, 1)
+
+    def passage_part(offset, cols):
+        ct = coef_t[pl.ds(lax.rem(z + offset, 4) * ROWS, ROWS), :]
+        part = mm(ct[:, 0:ROWS], QX[me_rows, cols]) + mm(ct[:, ROWS : 2 * ROWS], QX[par_rows, cols])
+        return part * LOGIT_SCALE
+
+    def rs(src, dst, i, step, start, length):
+        return pltpu.make_async_remote_copy(
+            src.at[:, pl.ds(start, length)], dst.at[:, pl.ds(start, length)], rs_send.at[i], rs_recv.at[i],
+            device_id=dev(0, 0, step, 0), device_id_type=MESH,
+        )
+
+    far_up = rs(rs_a, rr_a, 0, 1, 0, HD)
+    far_dn = rs(rs_a, rr_a, 1, 3, HD, HD)
+    up_free = rs(rs_up, rr_up, 2, 1, HD, HD)
+    dn_free = rs(rs_dn, rr_dn, 3, 3, 0, HD)
+    up_last = rs(rs_up, rr_up, 4, 1, 0, HD)
+    dn_last = rs(rs_dn, rr_dn, 5, 3, HD, HD)
+
+    def far(cols):
+        rs_a[:, cols] = passage_part(2, cols).astype(BF16)
+
+    tiles(0, HD, far)
+    far_up.start()
+    tiles(HD, HD, far)
+    far_dn.start()
+
     for dx in range(4):
         row = pick(codes_q(dx), hard_coef)
         cx_s[dx] = row
@@ -365,41 +438,6 @@
     for dx in range(1, 4):
         x_peer(cx_s, cx_r, cx_send, cx_recv, dx).start()
 
-    def half_coef(acc, pos, row_lse, out, column):
-        f = jnp.exp(acc[...] * LOGIT_SCALE - row_lse) - jnp.where(lane_p == pos, 1.0, 0.0)
-        out[...] = f.astype(BF16)
-        coef_t[:, column * ROWS : (column + 1) * ROWS] = jnp.transpose(f).astype(BF16)
-
-    half_coef(s_own, pos_own, lse, coef_o, 0)
-    pair(lse_s, lse_r, 1).wait_recv()
-    half_coef(s_par, pos_par, lse_r[:, 0:1], coef_p, 1)
-
-    def passage_part(offset, cols):
-        ct = coef_t[pl.ds(lax.rem(z + offset, 4) * ROWS, ROWS), :]
-        part = mm(ct[:, 0:ROWS], QX[me_rows, cols]) + mm(ct[:, ROWS : 2 * ROWS], QX[par_rows, cols])
-        return part * LOGIT_SCALE
-
-    def rs(src, dst, i, step, start, length):
-        return pltpu.make_async_remote_copy(
-            src.at[:, pl.ds(start, length)], dst.at[:, pl.ds(start, length)], rs_send.at[i], rs_recv.at[i],
-            device_id=dev(0, 0, step, 0), device_id_type=MESH,
-        )
-
-    far_up = rs(rs_a, rr_a, 0, 1, 0, HD)
-    far_dn = rs(rs_a, rr_a, 1, 3, HD, HD)
-    up_free = rs(rs_up, rr_up, 2, 1, HD, HD)
-    dn_free = rs(rs_dn, rr_dn, 3, 3, 0, HD)
-    up_last = rs(rs_up, rr_up, 4, 1, 0, HD)
-    dn_last = rs(rs_dn, rr_dn, 5, 3, HD, HD)
-
-    def far(cols):
-        rs_a[:, cols] = passage_part(2, cols).astype(BF16)
-
-    tiles(0, HD, far)
-    far_up.start()
-    tiles(HD, HD, far)
-    far_dn.start()
-
     def partner_part(cols):
         gx_s[:, cols] = (mm(coef_p[...], PZ[:, cols]) * LOGIT_SCALE).astype(BF16)
 
@@ -419,11 +457,13 @@
 
     for dx in range(1, 4):
         x_peer(cx_s, cx_r, cx_send, cx_recv, dx).wait_recv()
-    c_row = cx_r[0] + cx_r[1] + cx_r[2] + cx_r[3]
-    both = jnp.where(iota((2, S), 0) == 0, c_row, j_all)
-    c_s[0] = both
-    c_r[0] = both
-    spread(1, c_s, c_r, 1)
+    both = jnp.where(iota((2, S), 0) == 0, cx_r[0] + cx_r[1] + cx_r[2] + cx_r[3], j_all)
+    cz_s[0] = both
+    cz_r[0] = both
+    for dz in (1, 3, 2):
+        z_peer(dz).start()
+    for ch in range(len(EARLY), NCH):
+        second(ch)
 
     far_up.wait_recv()
 
@@ -439,6 +479,14 @@
 
     tiles(HD, HD, dn_sum)
     dn_last.start()
+
+    for dz in range(1, 4):
+        z_peer(dz).wait_recv()
+    both = fold(cz_r, r_a)
+    c_s[0] = both
+    c_r[0] = both
+    for m in range(1, NY * NC):
+        yc_peer(m).start()
 
     h = jnp.zeros((ROWS, S), F32)
     for k in range(3):
@@ -454,14 +502,14 @@
     gq_out = pltpu.make_async_copy(gq_ref, gq_hbm, out_sem.at[0])
     gq_out.start()
 
-    spread_all(c_r, 1).wait_recv()
-    both = fold(c_r)
+    yc_all().wait_recv()
+    both = fold(c_r, r_y * NC + r_c)
     hmat[...] = jnp.where(query_number == both[1:2, :], both[0:1, :], 0.0).astype(BF16)
     for ch in range(NCH):
         hard_all(1, ch).wait_recv()
 
         def passage_grad(cols):
-            gp_ref[:, cols] = passage_part(0, cols) + LOGIT_SCALE * mm(hmat[...], RQ[:, cols])
+            gp_ref[:, cols] = passage_part(0, cols) + LOGIT_SCALE * mm(hmat[...], RQ[:, :, cols].reshape(S, TN))
 
         tiles(ch * DC, DC, passage_grad)
     up_free.wait_recv()
@@ -484,11 +532,15 @@
             for kind in range(4):
                 ring(which, kind, ch).wait_send()
             hard_all(which, ch).wait_send()
+        for dz in range(1, 4):
+            turn(dz, ch).wait_send()
     for dx in range(1, 4):
         x_peer(xt_s, xt_r, xt_send, xt_recv, dx).wait_send()
         x_peer(cx_s, cx_r, cx_send, cx_recv, dx).wait_send()
-    spread_all(w_r, 0).wait_send()
-    spread_all(c_r, 1).wait_send()
+    for dz in range(1, 4):
+        z_peer(dz).wait_send()
+    asked().wait_send()
+    yc_all().wait_send()
     pair(st_s, st_r, 0).wait_send()
     pair(lse_s, lse_r, 1).wait_send()
     pair(gx_s, gx_r, 2).wait_send()
@@ -527,7 +579,8 @@
         out_specs=(vmem_spec, any_spec, any_spec),
         scratch_shapes=[
             vmem((4 * ROWS, D), BF16), vmem((4 * ROWS, D), BF16),
-            vmem((S, D), BF16), vmem((S, D), BF16), vmem((S, D), BF16), vmem((S, D), BF16),
+            vmem((S, D), BF16), vmem((4, S // 4, D), BF16), vmem((S, D), BF16), vmem((4, S // 4, D), BF16),
+            vmem((4, S // 4, D), BF16),
             wide, wide, wide, wide, wide, wide, wide, wide,
             vmem((ROWS, 4 * ROWS), F32), vmem((ROWS, 4 * ROWS), F32), vmem((ROWS, S), F32),
             vmem((2, S, 4 * ROWS), BF16),
@@ -536,11 +589,12 @@
             vmem((4, 2, S), F32), vmem((4, 2, S), F32),
             vmem((1, 1, S), F32), vmem((R, 1, S), F32),
             vmem((4, 1, S), F32), vmem((4, 1, S), F32),
-            vmem((1, 2, S), F32), vmem((R, 2, S), F32),
+            vmem((1, 2, S), F32), vmem((4, 2, S), F32),
+            vmem((1, 2, S), F32), vmem((NY * NC, 2, S), F32),
             vmem((ROWS, 128), F32), vmem((ROWS, 128), F32), vmem((ROWS, 128), F32), vmem((ROWS, 128), F32),
             vmem((ROWS, D), F32), vmem((ROWS, D), F32),
             dma((2,)), dma((5,)), dma((2, 4, NCH)), dma((2, 4, NCH)), dma((2, NCH)), dma((2, NCH)),
-            dma((4,)), dma((4,)), dma((4,)), dma((4,)), dma((2,)), dma((2,)), dma((3,)), dma((3,)),
+            dma((4,)), dma((4,)), dma((4,)), dma((4,)), dma((4,)), dma((4,)), dma((4, NCH)), dma((4, NCH)), dma((2,)), dma((2,)), dma((3,)), dma((3,)),
             dma((6,)), dma((6,)),
         ],
         compiler_params=pltpu.CompilerParams(

time: 166 us -> 147 us (0.89)
  Pallas kernels: 165 us -> 146 us
    pallas_call x1, Pallas kernels: 160 us -> 142 us  [on_device(): pl.pallas_call(functools.partial(kernel, NY, NC, D, shift), out_shape=(ja...]
where the time goes in v3:
time: 147 us
  Pallas kernels  146 us (99%)
    pallas_call x1, Pallas kernels, on_device(): pl.pallas_call(functools.partial(kernel, NY, NC, D, shift), out_shape=(ja...  142 us
    pallas_call x1, Pallas kernels, on_device(): pl.pallas_call(results, grid=(4,), in_specs=[row, block, block], out_spec...  4.7 us

profile of v3, /device:TPU:1, one launch (start us, length us, event | category | flops | bytes accessed | tf_op | source)
XLA Modules:
  0.0 146.9 jit_solution(6668525500487793129)
XLA Ops:
  0.6 141.5 %infonce.1 = (f32[1,128]{1,0:T(1,128)}, f32[128,4096]{1,0:T(8,128)}, f32[128,4096]{1,0:T(8,128)}) custom-call(bf16[128,4096]{1,0:T(8,128)(2,1)} %q_hbm.1, bf16[128,4096]{1,0:T(8,128)(2,1)} %p_hbm.1, s32[1,128]{1,0:T(1,128)} %pos_ref.1, s32[3,128]{1,0:T(4,128)} %bitcast.3, s32[3,128]{1,0:T(4,128)} %bitcast.4), custom_call_target="tpu_custom_call" | custom-call | flops 8999999488 | bytes 8388608 | tf_op jit(solution)/shard_map/infonce/pallas_call | solution.py:571
  142.2 4.7 %results.1 = (f32[1,128]{1,0:T(1,128)}, f32[128,4096]{1,0:T(8,128)}, f32[128,4096]{1,0:T(8,128)}) custom-call(f32[1,128]{1,0:T(1,128)} %get-tuple-element.9.loss_in, f32[128,4096]{1,0:T(8,128)} %get-tuple-element.10.gq_in, f32[128,4096]{1,0:T(8,128)} %get-tuple-element.11.gp_in), custom_call_target="tpu_custom_call" | custom-call | tf_op jit(solution)/shard_map/results/pallas_call | solution.py:608

commit v4 on v3

--- a/solution.py
+++ b/solution.py
@@ -47,15 +47,16 @@
     NY, NC, D, shift,
     q_hbm, p_hbm, pos_ref, own_ref, row_ref,
     loss_ref, gq_hbm, gp_hbm,
-    PZ, QX, SP, SQ, RP, MQ, RQ,
+    PZ, QX, SP, SQ, MP, RP, MQ, RQ,
     rs_a, rs_up, rs_dn, rr_a, rr_up, rr_dn, gx_s, gx_r,
     s_own, s_par, hs, gather, coef_o, coef_p, coef_t, hmat,
     xt_s, xt_r, w_s, w_r, cx_s, cx_r, cz_s, cz_r, c_s, c_r, st_s, st_r, lse_s, lse_r, gq_ref, gp_ref,
     in_sem, out_sem, ag_send, ag_recv, hard_send, hard_recv,
-    xt_send, xt_recv, cx_send, cx_recv, cz_send, cz_recv, turn_send, turn_recv, small_send, small_recv, pair_send, pair_recv, rs_send, rs_recv,
+    xt_send, xt_recv, cx_send, cx_recv, cz_send, cz_recv, turn_send, turn_recv, yc_send, yc_recv, pair_send, pair_recv, rs_send, rs_recv,
 ):
     R = 4 * NY * NC
     S = 16 * R
+    YC = NY * NC
     HR = S // 4
     SECOND = [0] + sorted(range(1, NY * NC), key=lambda m: (m % NC, m // NC == 2, m))
     DC = D // NCH
@@ -77,32 +78,17 @@
         c2 = lax.rem(c + dc, NC)
         return ((y2 * 2 + lax.rem(x2, 2)) * NC + c2, (x2 // 2) * 4 + z2)
 
-    def order(n):
-        cc = lax.rem(n, NC)
-        i = lax.rem(n // NC, 4)
-        s = n // (4 * NC)
-        a = lax.rem(1 + 2 * i + i // 2, 4)
-        yy = lax.rem(a + s + 1, NY)
-        return a, yy, cc, (a * NY + yy) * NC + cc
-
     p_in = pltpu.make_async_copy(p_hbm, PZ.at[pl.ds(z * ROWS, ROWS)], in_sem.at[0])
     q_in = pltpu.make_async_copy(q_hbm, QX.at[pl.ds(x * ROWS, ROWS)], in_sem.at[1])
     p_in.start()
     q_in.start()
     barrier = pltpu.get_barrier_semaphore()
 
-    def greet(n, carry):
-        a, yy, cc, r = order(n)
-
-        @pl.when(r > 0)
-        def _():
-            pl.semaphore_signal(barrier, inc=1, device_id=dev(a, yy, 0, cc), device_id_type=MESH)
-
-        return carry
-
-    lax.fori_loop(0, R, greet, 0)
-    for dz in range(1, 4):
-        pl.semaphore_signal(barrier, inc=1, device_id=dev(0, 0, dz, 0), device_id_type=MESH)
+    for n in range(1, 4):
+        pl.semaphore_signal(barrier, inc=1, device_id=dev(n, 0, 0, 0), device_id_type=MESH)
+        pl.semaphore_signal(barrier, inc=1, device_id=dev(0, 0, n, 0), device_id_type=MESH)
+    for m in range(1, YC):
+        pl.semaphore_signal(barrier, inc=1, device_id=dev(0, m // NC, 0, m % NC), device_id_type=MESH)
     lane = iota((1, S), 1)
     slot_r = lane // 16
     slot_b = lax.rem(lane, 16) // 4
@@ -139,19 +125,20 @@
         return jnp.sum(total, axis=0, keepdims=True)
 
     w_row = pick(codes_p, hrow)
-    w_s[0] = w_row
-    w_r[0] = w_row
     query_number = iota((ROWS, 1), 0).astype(F32)
     query_and_row = [query_number + ROWS * hrow[k] for k in range(3)]
     pos_row = pos_ref[...].astype(F32)
     pos_wide = jnp.concatenate([pos_row] + [jnp.zeros((1, S - ROWS), F32)], axis=1)
+    sub4 = iota((4, S), 0)
     for dx in range(4):
-        table = jnp.where(iota((2, S), 0) == 0, pick(codes_q(dx), query_and_row), pos_wide)
+        table = jnp.where(
+            sub4 == 0, pick(codes_q(dx), query_and_row), jnp.where(sub4 == 1, pos_wide, jnp.where(sub4 == 2, w_row, 0.0))
+        )
         xt_s[dx] = table
         if dx == 0:
             xt_r[0] = table
 
-    pl.semaphore_wait(barrier, R - 1 + 3)
+    pl.semaphore_wait(barrier, 6 + YC - 1)
     p_in.wait()
     q_in.wait()
 
@@ -187,39 +174,24 @@
             ring(which, 0, ch).start()
             ring(which, 1, ch).start()
 
-    def ask(n, carry):
-        a, yy, cc, r = order(n)
-
-        @pl.when(r > 0)
-        def _():
-            target = dev(lax.rem(4 - a, 4), lax.rem(NY - yy, NY), 0, lax.rem(NC - cc, NC))
-            pltpu.make_async_remote_copy(
-                w_s.at[0], w_r.at[r], small_send.at[0], small_recv.at[0], device_id=target, device_id_type=MESH
-            ).start()
-
-        return carry
-
-    def asked():
-        ref = w_r.at[pl.ds(1, R - 1)]
-        return pltpu.make_async_remote_copy(
-            ref, ref, small_send.at[0], small_recv.at[0], device_id=dev(1, 0, 0, 0), device_id_type=MESH
-        )
-
     def z_peer(dz):
         return pltpu.make_async_remote_copy(
             cz_s.at[0], cz_r.at[dz], cz_send.at[dz], cz_recv.at[dz], device_id=dev(0, 0, dz, 0), device_id_type=MESH
         )
 
-    def yc_peer(m):
-        return pltpu.make_async_remote_copy(
-            c_s.at[0], c_r.at[m], small_send.at[1], small_recv.at[1],
-            device_id=dev(0, m // NC, 0, m % NC), device_id_type=MESH,
-        )
-
-    def yc_all():
-        ref = c_r.at[pl.ds(1, NY * NC - 1)]
-        return pltpu.make_async_remote_copy(
-            ref, ref, small_send.at[1], small_recv.at[1], device_id=dev(1, 0, 0, 0), device_id_type=MESH
+    def yc_peer(kind, m):
+        dy, dc = m // NC, m % NC
+        if kind == 0:
+            dy, dc = (NY - dy) % NY, (NC - dc) % NC
+        src, dst = ((w_s, w_r), (c_s, c_r))[kind]
+        return pltpu.make_async_remote_copy(
+            src.at[0], dst.at[m], yc_send.at[kind], yc_recv.at[kind], device_id=dev(0, dy, 0, dc), device_id_type=MESH
+        )
+
+    def yc_all(kind):
+        ref = (w_r, c_r)[kind].at[pl.ds(1, YC - 1)]
+        return pltpu.make_async_remote_copy(
+            ref, ref, yc_send.at[kind], yc_recv.at[kind], device_id=dev(1, 0, 0, 0), device_id_type=MESH
         )
 
     def fold(ref, group):
@@ -229,8 +201,6 @@
             total = total + jnp.where(group == n, values[n], 0.0)
         return total
 
-    slot_number = slot_r
-
     def x_peer(src, dst, send, recv, dx):
         return pltpu.make_async_remote_copy(
             src.at[dx], dst.at[dx], send.at[dx], recv.at[dx], device_id=dev(dx, 0, 0, 0), device_id_type=MESH
@@ -241,46 +211,42 @@
         want = to_column(index).astype(jnp.int32) + lax.rem(n, 16) // 4 * ROWS
         gather[slot] = (want == iota((S, 4 * ROWS), 1)).astype(BF16)
 
-    def hard_starts(ch):
-        def body(n, carry):
-            a, yy, cc, r = order(n)
-
-            @pl.when(r > 0)
-            def _():
-                pltpu.make_async_remote_copy(
-                    SP.at[pl.ds(r * 16, 16), pl.ds(ch * DC, DC)], RP.at[pl.ds(r * 16, 16), pl.ds(ch * DC, DC)],
-                    hard_send.at[0, ch], hard_recv.at[0, ch], device_id=dev(a, yy, 0, cc), device_id_type=MESH,
-                ).start()
-
-            return carry
-
-        lax.fori_loop(0, R, body, 0)
-
-    def hard_all(kind, ch):
+    def hard_starts(kind, ch):
+        src, dst = ((SP, MP), (MQ, RQ))[kind]
         cols = pl.ds(ch * DC, DC)
-        ref = RP.at[pl.ds(16, S - 16), cols] if kind == 0 else RQ.at[:, pl.ds(16, HR - 16), cols]
-        return pltpu.make_async_remote_copy(
-            ref, ref, hard_send.at[kind, ch], hard_recv.at[kind, ch], device_id=dev(1, 0, 0, 0), device_id_type=MESH
-        )
-
-    def turn(dz, ch):
-        cols = pl.ds(ch * DC, DC)
-        return pltpu.make_async_remote_copy(
-            SQ.at[dz, :, cols], MQ.at[dz, :, cols], turn_send.at[dz, ch], turn_recv.at[dz, ch],
-            device_id=dev(0, 0, dz, 0), device_id_type=MESH,
-        )
-
-    def second(ch):
-        cols = pl.ds(ch * DC, DC)
-        for dz in range(1, 4):
-            turn(dz, ch).wait_recv()
         for m in SECOND[1:]:
             part = pl.ds(m * 16, 16)
             pltpu.make_async_remote_copy(
-                MQ.at[:, part, cols], RQ.at[:, part, cols], hard_send.at[1, ch], hard_recv.at[1, ch],
+                src.at[:, part, cols], dst.at[:, part, cols], hard_send.at[kind, ch], hard_recv.at[kind, ch],
                 device_id=dev(0, m // NC, 0, m % NC), device_id_type=MESH,
             ).start()
-        RQ[:, 0:16, cols] = MQ[:, 0:16, cols]
+        dst[:, 0:16, cols] = src[:, 0:16, cols]
+
+    def hard_all(kind, ch):
+        ref = (MP, RQ)[kind].at[:, pl.ds(16, HR - 16), pl.ds(ch * DC, DC)]
+        return pltpu.make_async_remote_copy(
+            ref, ref, hard_send.at[kind, ch], hard_recv.at[kind, ch], device_id=dev(1, 0, 0, 0), device_id_type=MESH
+        )
+
+    def turn(kind, n, ch):
+        cols = pl.ds(ch * DC, DC)
+        src, dst = ((MP, RP), (SQ, MQ))[kind]
+        return pltpu.make_async_remote_copy(
+            src.at[n, :, cols], dst.at[n, :, cols], turn_send.at[kind, n, ch], turn_recv.at[kind, n, ch],
+            device_id=dev(n, 0, 0, 0) if kind == 0 else dev(0, 0, n, 0), device_id_type=MESH,
+        )
+
+    def deliver(ch):
+        cols = pl.ds(ch * DC, DC)
+        hard_all(0, ch).wait_recv()
+        for n in (1, 3, 2):
+            turn(0, n, ch).start()
+        RP[0, :, cols] = MP[0, :, cols]
+
+    def second(ch):
+        for n in range(1, 4):
+            turn(1, n, ch).wait_recv()
+        hard_starts(1, ch)
 
     def tiles(start, length, body):
         def step(t, carry):
@@ -291,8 +257,8 @@
 
     def serve_p(cols):
         rows = mm(gather[0], PZ[:, cols]).astype(BF16)
-        SP[:, cols] = rows
-        RP[0:16, cols] = rows[0:16]
+        for n in range(4):
+            SP[n, :, cols] = rows[n * HR : (n + 1) * HR]
 
     def serve_q(cols):
         rows = mm(gather[1], QX[:, cols]).astype(BF16)
@@ -318,19 +284,25 @@
                 ring(which, kind + 2, ch).start()
 
     own_sends(0)
-    lax.fori_loop(0, R, ask, 0)
     for dx in range(1, 4):
         x_peer(xt_s, xt_r, xt_send, xt_recv, dx).start()
     own_sends(1)
-    asked().wait_recv()
-    gather_matrix(fold(w_r, slot_number), 0)
-    forward(0)
-    own_sends(2)
     for dx in range(1, 4):
         x_peer(xt_s, xt_r, xt_send, xt_recv, dx).wait_recv()
     tables = (xt_r[0] + xt_r[1] + xt_r[2] + xt_r[3])[0:1, :].astype(jnp.int32)
+    wanted = jnp.zeros((1, S), F32)
+    for dx in range(4):
+        wanted = wanted + jnp.where(r_a == (4 - dx) % 4, xt_r[dx][2:3, :], 0.0)
+    w_s[0] = wanted
+    w_r[0] = wanted
+    for m in range(1, YC):
+        yc_peer(0, m).start()
     j_all = (tables // ROWS).astype(F32)
+    forward(0)
+    own_sends(2)
     gather_matrix(lax.rem(tables, ROWS).astype(F32), 1)
+    yc_all(0).wait_recv()
+    gather_matrix(fold(w_r, r_y * NC + r_c), 0)
 
     for ch in range(NCH):
         if ch + 1 < NCH:
@@ -340,14 +312,20 @@
         arriving(0, 2, ch).wait_recv()
         arriving(0, 3, ch).wait_recv()
         tiles(ch * DC, DC, serve_p)
-        hard_starts(ch)
+        hard_starts(0, ch)
+        if ch > 0:
+            deliver(ch - 1)
         arriving(1, 2, ch).wait_recv()
         arriving(1, 3, ch).wait_recv()
         tiles(ch * DC, DC, serve_q)
         for dz in (1, 3, 2):
-            turn(dz, ch).start()
+            turn(1, dz, ch).start()
         score(s_own, me_rows, PZ, ch)
         score(s_par, par_rows, PZ, ch)
+    deliver(NCH - 1)
+
+    def hard_score(cols):
+        hs[...] += mm_t(QX[me_rows, cols], RP[:, :, cols].reshape(S, TN))
 
     base = (xh * 4 * ROWS).astype(F32)
     lane_p = iota((ROWS, 4 * ROWS), 1).astype(F32)
@@ -374,8 +352,9 @@
     m_o, l_o, sp_o = half_stats(s_own, pos_own)
 
     for ch in range(NCH):
-        hard_all(0, ch).wait_recv()
-        score(hs, me_rows, RP, ch)
+        for n in range(1, 4):
+            turn(0, n, ch).wait_recv()
+        tiles(ch * DC, DC, hard_score)
         if ch in EARLY:
             second(EARLY.index(ch))
     pair(st_s, st_r, 0).wait_recv()
@@ -485,8 +464,8 @@
     both = fold(cz_r, r_a)
     c_s[0] = both
     c_r[0] = both
-    for m in range(1, NY * NC):
-        yc_peer(m).start()
+    for m in range(1, YC):
+        yc_peer(1, m).start()
 
     h = jnp.zeros((ROWS, S), F32)
     for k in range(3):
@@ -495,14 +474,14 @@
     pair(gx_s, gx_r, 2).wait_recv()
 
     def query_grad(cols):
-        part = mm(coef_o[...], PZ[:, cols]) + mm(hmat[...], RP[:, cols])
+        part = mm(coef_o[...], PZ[:, cols]) + mm(hmat[...], RP[:, :, cols].reshape(S, TN))
         gq_ref[:, cols] = part * LOGIT_SCALE + gx_r[:, cols].astype(F32)
 
     tiles(0, D, query_grad)
     gq_out = pltpu.make_async_copy(gq_ref, gq_hbm, out_sem.at[0])
     gq_out.start()
 
-    yc_all().wait_recv()
+    yc_all(1).wait_recv()
     both = fold(c_r, r_y * NC + r_c)
     hmat[...] = jnp.where(query_number == both[1:2, :], both[0:1, :], 0.0).astype(BF16)
     for ch in range(NCH):
@@ -532,15 +511,16 @@
             for kind in range(4):
                 ring(which, kind, ch).wait_send()
             hard_all(which, ch).wait_send()
-        for dz in range(1, 4):
-            turn(dz, ch).wait_send()
+        for n in range(1, 4):
+            turn(0, n, ch).wait_send()
+            turn(1, n, ch).wait_send()
     for dx in range(1, 4):
         x_peer(xt_s, xt_r, xt_send, xt_recv, dx).wait_send()
         x_peer(cx_s, cx_r, cx_send, cx_recv, dx).wait_send()
     for dz in range(1, 4):
         z_peer(dz).wait_send()
-    asked().wait_send()
-    yc_all().wait_send()
+    yc_all(0).wait_send()
+    yc_all(1).wait_send()
     pair(st_s, st_r, 0).wait_send()
     pair(lse_s, lse_r, 1).wait_send()
     pair(gx_s, gx_r, 2).wait_send()
@@ -566,6 +546,7 @@
     vmem = pltpu.VMEM
     dma = pltpu.SemaphoreType.DMA
     wide = vmem((ROWS, D), BF16)
+    parts = vmem((4, S // 4, D), BF16)
     any_spec = pl.BlockSpec(memory_space=pl.ANY)
     vmem_spec = pl.BlockSpec(memory_space=pltpu.VMEM)
     loss, gq, gp = pl.pallas_call(
@@ -579,22 +560,21 @@
         out_specs=(vmem_spec, any_spec, any_spec),
         scratch_shapes=[
             vmem((4 * ROWS, D), BF16), vmem((4 * ROWS, D), BF16),
-            vmem((S, D), BF16), vmem((4, S // 4, D), BF16), vmem((S, D), BF16), vmem((4, S // 4, D), BF16),
-            vmem((4, S // 4, D), BF16),
+            parts, parts, parts, parts, parts, parts,
             wide, wide, wide, wide, wide, wide, wide, wide,
             vmem((ROWS, 4 * ROWS), F32), vmem((ROWS, 4 * ROWS), F32), vmem((ROWS, S), F32),
             vmem((2, S, 4 * ROWS), BF16),
             vmem((ROWS, 4 * ROWS), BF16), vmem((ROWS, 4 * ROWS), BF16), vmem((4 * ROWS, 2 * ROWS), BF16),
             vmem((ROWS, S), BF16),
-            vmem((4, 2, S), F32), vmem((4, 2, S), F32),
-            vmem((1, 1, S), F32), vmem((R, 1, S), F32),
+            vmem((4, 4, S), F32), vmem((4, 4, S), F32),
+            vmem((1, 1, S), F32), vmem((NY * NC, 1, S), F32),
             vmem((4, 1, S), F32), vmem((4, 1, S), F32),
             vmem((1, 2, S), F32), vmem((4, 2, S), F32),
             vmem((1, 2, S), F32), vmem((NY * NC, 2, S), F32),
             vmem((ROWS, 128), F32), vmem((ROWS, 128), F32), vmem((ROWS, 128), F32), vmem((ROWS, 128), F32),
             vmem((ROWS, D), F32), vmem((ROWS, D), F32),
             dma((2,)), dma((5,)), dma((2, 4, NCH)), dma((2, 4, NCH)), dma((2, NCH)), dma((2, NCH)),
-            dma((4,)), dma((4,)), dma((4,)), dma((4,)), dma((4,)), dma((4,)), dma((4, NCH)), dma((4, NCH)), dma((2,)), dma((2,)), dma((3,)), dma((3,)),
+            dma((4,)), dma((4,)), dma((4,)), dma((4,)), dma((4,)), dma((4,)), dma((2, 4, NCH)), dma((2, 4, NCH)), dma((2,)), dma((2,)), dma((3,)), dma((3,)),
             dma((6,)), dma((6,)),
         ],
         compiler_params=pltpu.CompilerParams(
@@ -603,11 +583,11 @@
         cost_estimate=pl.CostEstimate(flops=9 * 10**9, bytes_accessed=8 * 2**20, transcendentals=2 * 10**5),
         name="infonce",
     )(queries, passages, positives, hard_owner.T, hard_row.T)
-    block = pl.BlockSpec((ROWS // 4, D), lambda i: (i, 0))
+    block = pl.BlockSpec((ROWS // 2, D), lambda i: (i, 0))
     row = pl.BlockSpec((1, ROWS), lambda i: (0, 0))
     loss, gq, gp = pl.pallas_call(
         results,
-        grid=(4,),
+        grid=(2,),
         in_specs=[row, block, block],
         out_specs=(row, block, block),
         out_shape=tuple(jax.ShapeDtypeStruct(a.shape, F32) for a in (loss, gq, gp)),

time: 147 us -> 142 us (0.966)
  Pallas kernels: 146 us -> 141 us
    pallas_call x1, Pallas kernels: 142 us -> 138 us  [on_device(): pl.pallas_call(functools.partial(kernel, NY, NC, D, shift), out_shape=(ja...]
where the time goes in v4:
time: 142 us
  Pallas kernels  141 us (99%)
    pallas_call x1, Pallas kernels, on_device(): pl.pallas_call(functools.partial(kernel, NY, NC, D, shift), out_shape=(ja...  138 us
    pallas_call x1, Pallas kernels, on_device(): pl.pallas_call(results, grid=(2,), in_specs=[row, block, block], out_spec...  3.7 us

profile of v4, /device:TPU:1, one launch (start us, length us, event | category | flops | bytes accessed | tf_op | source)
XLA Modules:
  0.0 142.0 jit_solution(97940972746419897)
XLA Ops:
  0.6 137.7 %infonce.1 = (f32[1,128]{1,0:T(1,128)}, f32[128,4096]{1,0:T(8,128)}, f32[128,4096]{1,0:T(8,128)}) custom-call(bf16[128,4096]{1,0:T(8,128)(2,1)} %q_hbm.1, bf16[128,4096]{1,0:T(8,128)(2,1)} %p_hbm.1, s32[1,128]{1,0:T(1,128)} %pos_ref.1, s32[3,128]{1,0:T(4,128)} %bitcast.3, s32[3,128]{1,0:T(4,128)} %bitcast.4), custom_call_target="tpu_custom_call" | custom-call | flops 8999999488 | bytes 8388608 | tf_op jit(solution)/shard_map/infonce/pallas_call | solution.py:552
  138.3 3.7 %results.1 = (f32[1,128]{1,0:T(1,128)}, f32[128,4096]{1,0:T(8,128)}, f32[128,4096]{1,0:T(8,128)}) custom-call(f32[1,128]{1,0:T(1,128)} %get-tuple-element.9.loss_in, f32[128,4096]{1,0:T(8,128)} %get-tuple-element.10.gq_in, f32[128,4096]{1,0:T(8,128)} %get-tuple-element.11.gp_in), custom_call_target="tpu_custom_call" | custom-call | tf_op jit(solution)/shard_map/results/pallas_call | solution.py:588

commit v5 on v4

--- a/solution.py
+++ b/solution.py
@@ -12,7 +12,7 @@
 ROWS = 128
 CAP = 4
 NCH = 4
-EARLY = (1, 2)
+EARLY = (1, 2, 3)
 NEG = -1e30
 MESH = pl.DeviceIdType.MESH
 F32 = jnp.float32
@@ -46,9 +46,9 @@
 def kernel(
     NY, NC, D, shift,
     q_hbm, p_hbm, pos_ref, own_ref, row_ref,
-    loss_ref, gq_hbm, gp_hbm,
+    loss_ref, gq_hbm, gp_hbm, rr_up, rr_dn, gx_r,
     PZ, QX, SP, SQ, MP, RP, MQ, RQ,
-    rs_a, rs_up, rs_dn, rr_a, rr_up, rr_dn, gx_s, gx_r,
+    rs_a, rs_up, rs_dn, rr_a, gx_s,
     s_own, s_par, hs, gather, coef_o, coef_p, coef_t, hmat,
     xt_s, xt_r, w_s, w_r, cx_s, cx_r, cz_s, cz_r, c_s, c_r, st_s, st_r, lse_s, lse_r, gq_ref, gp_ref,
     in_sem, out_sem, ag_send, ag_recv, hard_send, hard_recv,
@@ -374,41 +374,6 @@
     loss_ref[...] = to_row(lse - (sp_o + sp_r))
     hard_coef = [jnp.exp(present[k] - lse) for k in range(3)]
 
-    def half_coef(acc, pos, row_lse, out, column):
-        f = jnp.exp(acc[...] * LOGIT_SCALE - row_lse) - jnp.where(lane_p == pos, 1.0, 0.0)
-        out[...] = f.astype(BF16)
-        coef_t[:, column * ROWS : (column + 1) * ROWS] = jnp.transpose(f).astype(BF16)
-
-    half_coef(s_own, pos_own, lse, coef_o, 0)
-    pair(lse_s, lse_r, 1).wait_recv()
-    half_coef(s_par, pos_par, lse_r[:, 0:1], coef_p, 1)
-
-    def passage_part(offset, cols):
-        ct = coef_t[pl.ds(lax.rem(z + offset, 4) * ROWS, ROWS), :]
-        part = mm(ct[:, 0:ROWS], QX[me_rows, cols]) + mm(ct[:, ROWS : 2 * ROWS], QX[par_rows, cols])
-        return part * LOGIT_SCALE
-
-    def rs(src, dst, i, step, start, length):
-        return pltpu.make_async_remote_copy(
-            src.at[:, pl.ds(start, length)], dst.at[:, pl.ds(start, length)], rs_send.at[i], rs_recv.at[i],
-            device_id=dev(0, 0, step, 0), device_id_type=MESH,
-        )
-
-    far_up = rs(rs_a, rr_a, 0, 1, 0, HD)
-    far_dn = rs(rs_a, rr_a, 1, 3, HD, HD)
-    up_free = rs(rs_up, rr_up, 2, 1, HD, HD)
-    dn_free = rs(rs_dn, rr_dn, 3, 3, 0, HD)
-    up_last = rs(rs_up, rr_up, 4, 1, 0, HD)
-    dn_last = rs(rs_dn, rr_dn, 5, 3, HD, HD)
-
-    def far(cols):
-        rs_a[:, cols] = passage_part(2, cols).astype(BF16)
-
-    tiles(0, HD, far)
-    far_up.start()
-    tiles(HD, HD, far)
-    far_dn.start()
-
     for dx in range(4):
         row = pick(codes_q(dx), hard_coef)
         cx_s[dx] = row
@@ -417,22 +382,35 @@
     for dx in range(1, 4):
         x_peer(cx_s, cx_r, cx_send, cx_recv, dx).start()
 
-    def partner_part(cols):
-        gx_s[:, cols] = (mm(coef_p[...], PZ[:, cols]) * LOGIT_SCALE).astype(BF16)
-
-    tiles(0, D, partner_part)
-    pair(gx_s, gx_r, 2).start()
-
-    def up_part(cols):
-        rs_up[:, cols] = passage_part(1, cols).astype(BF16)
-
-    def dn_part(cols):
-        rs_dn[:, cols] = passage_part(3, cols).astype(BF16)
-
-    tiles(HD, HD, up_part)
-    up_free.start()
-    tiles(0, HD, dn_part)
-    dn_free.start()
+    def half_coef(acc, pos, row_lse, out, column):
+        f = jnp.exp(acc[...] * LOGIT_SCALE - row_lse) - jnp.where(lane_p == pos, 1.0, 0.0)
+        out[...] = f.astype(BF16)
+        coef_t[:, column * ROWS : (column + 1) * ROWS] = jnp.transpose(f).astype(BF16)
+
+    half_coef(s_own, pos_own, lse, coef_o, 0)
+    pair(lse_s, lse_r, 1).wait_recv()
+    half_coef(s_par, pos_par, lse_r[:, 0:1], coef_p, 1)
+
+    def passage_part(offset, cols):
+        ct = coef_t[pl.ds(lax.rem(z + offset, 4) * ROWS, ROWS), :]
+        part = mm(ct[:, 0:ROWS], QX[me_rows, cols]) + mm(ct[:, ROWS : 2 * ROWS], QX[par_rows, cols])
+        return part * LOGIT_SCALE
+
+    def rs(src, dst, i, step, start, length):
+        return pltpu.make_async_remote_copy(
+            src.at[:, pl.ds(start, length)], dst.at[:, pl.ds(start, length)], rs_send.at[i], rs_recv.at[i],
+            device_id=dev(0, 0, step, 0), device_id_type=MESH,
+        )
+
+    far_up = rs(rs_a, rr_a, 0, 1, 0, HD)
+    far_dn = rs(rs_a, rr_a, 1, 3, HD, HD)
+    up_free = rs(rs_up, rr_up, 2, 1, HD, HD)
+    dn_free = rs(rs_dn, rr_dn, 3, 3, 0, HD)
+    up_last = rs(rs_up, rr_up, 4, 1, 0, HD)
+    dn_last = rs(rs_dn, rr_dn, 5, 3, HD, HD)
+
+    def far(cols):
+        rs_a[:, cols] = passage_part(2, cols).astype(BF16)
 
     for dx in range(1, 4):
         x_peer(cx_s, cx_r, cx_send, cx_recv, dx).wait_recv()
@@ -441,23 +419,22 @@
     cz_r[0] = both
     for dz in (1, 3, 2):
         z_peer(dz).start()
-    for ch in range(len(EARLY), NCH):
-        second(ch)
-
-    far_up.wait_recv()
-
-    def up_sum(cols):
-        rs_up[:, cols] = (passage_part(1, cols) + rr_a[:, cols].astype(F32)).astype(BF16)
-
-    tiles(0, HD, up_sum)
-    up_last.start()
-    far_dn.wait_recv()
-
-    def dn_sum(cols):
-        rs_dn[:, cols] = (passage_part(3, cols) + rr_a[:, cols].astype(F32)).astype(BF16)
-
-    tiles(HD, HD, dn_sum)
-    dn_last.start()
+    tiles(0, HD, far)
+    far_up.start()
+    tiles(HD, HD, far)
+    far_dn.start()
+
+    def partner_part(cols):
+        gx_s[:, cols] = (mm(coef_p[...], PZ[:, cols]) * LOGIT_SCALE).astype(BF16)
+
+    tiles(0, D, partner_part)
+    pair(gx_s, gx_r, 2).start()
+
+    def up_part(cols):
+        rs_up[:, cols] = passage_part(1, cols).astype(BF16)
+
+    def dn_part(cols):
+        rs_dn[:, cols] = passage_part(3, cols).astype(BF16)
 
     for dz in range(1, 4):
         z_peer(dz).wait_recv()
@@ -467,15 +444,37 @@
     for m in range(1, YC):
         yc_peer(1, m).start()
 
+    tiles(HD, HD, up_part)
+    up_free.start()
+    tiles(0, HD, dn_part)
+    dn_free.start()
+
+    for ch in range(len(EARLY), NCH):
+        second(ch)
+
+    far_up.wait_recv()
+
+    def up_sum(cols):
+        rs_up[:, cols] = (passage_part(1, cols) + rr_a[:, cols].astype(F32)).astype(BF16)
+
+    tiles(0, HD, up_sum)
+    up_last.start()
+    far_dn.wait_recv()
+
+    def dn_sum(cols):
+        rs_dn[:, cols] = (passage_part(3, cols) + rr_a[:, cols].astype(F32)).astype(BF16)
+
+    tiles(HD, HD, dn_sum)
+    dn_last.start()
+
     h = jnp.zeros((ROWS, S), F32)
     for k in range(3):
         h = h + jnp.where(mask[k], hard_coef[k], 0.0)
     hmat[...] = h.astype(BF16)
-    pair(gx_s, gx_r, 2).wait_recv()
 
     def query_grad(cols):
         part = mm(coef_o[...], PZ[:, cols]) + mm(hmat[...], RP[:, :, cols].reshape(S, TN))
-        gq_ref[:, cols] = part * LOGIT_SCALE + gx_r[:, cols].astype(F32)
+        gq_ref[:, cols] = (part * LOGIT_SCALE).astype(BF16)
 
     tiles(0, D, query_grad)
     gq_out = pltpu.make_async_copy(gq_ref, gq_hbm, out_sem.at[0])
@@ -488,23 +487,18 @@
         hard_all(1, ch).wait_recv()
 
         def passage_grad(cols):
-            gp_ref[:, cols] = passage_part(0, cols) + LOGIT_SCALE * mm(hmat[...], RQ[:, :, cols].reshape(S, TN))
+            total = passage_part(0, cols) + LOGIT_SCALE * mm(hmat[...], RQ[:, :, cols].reshape(S, TN))
+            gp_ref[:, cols] = total.astype(BF16)
 
         tiles(ch * DC, DC, passage_grad)
+    gp_out = pltpu.make_async_copy(gp_ref, gp_hbm, out_sem.at[1])
+    gp_out.start()
+    pair(gx_s, gx_r, 2).wait_recv()
     up_free.wait_recv()
     dn_free.wait_recv()
     up_last.wait_recv()
     dn_last.wait_recv()
-
-    def last(cols):
-        gp_ref[:, cols] += rr_up[:, cols].astype(F32) + rr_dn[:, cols].astype(F32)
-
-    outs = [gq_out]
-    for ch in range(4):
-        tiles(ch * D // 4, D // 4, last)
-        cols = pl.ds(ch * D // 4, D // 4)
-        outs.append(pltpu.make_async_copy(gp_ref.at[:, cols], gp_hbm.at[:, cols], out_sem.at[1 + ch]))
-        outs[-1].start()
+    outs = [gq_out, gp_out]
 
     for ch in range(NCH):
         for which in (0, 1):
@@ -530,10 +524,10 @@
         copy.wait()
 
 
-def results(loss_in, gq_in, gp_in, loss_out, gq_out, gp_out):
+def results(loss_in, gq_in, gp_in, up_in, dn_in, gx_in, loss_out, gq_out, gp_out):
     loss_out[...] = loss_in[...]
-    gq_out[...] = gq_in[...]
-    gp_out[...] = gp_in[...]
+    gq_out[...] = gq_in[...].astype(F32) + gx_in[...].astype(F32)
+    gp_out[...] = gp_in[...].astype(F32) + up_in[...].astype(F32) + dn_in[...].astype(F32)
 
 
 def on_device(ngrp, queries, passages, positives, hard_owner, hard_row):
@@ -549,19 +543,22 @@
     parts = vmem((4, S // 4, D), BF16)
     any_spec = pl.BlockSpec(memory_space=pl.ANY)
     vmem_spec = pl.BlockSpec(memory_space=pltpu.VMEM)
-    loss, gq, gp = pl.pallas_call(
+    loss, gq, gp, up, dn, gx = pl.pallas_call(
         functools.partial(kernel, NY, NC, D, shift),
         out_shape=(
             jax.ShapeDtypeStruct((1, ROWS), F32),
-            jax.ShapeDtypeStruct((ROWS, D), F32),
-            jax.ShapeDtypeStruct((ROWS, D), F32),
+            jax.ShapeDtypeStruct((ROWS, D), BF16),
+            jax.ShapeDtypeStruct((ROWS, D), BF16),
+            jax.ShapeDtypeStruct((ROWS, D), BF16),
+            jax.ShapeDtypeStruct((ROWS, D), BF16),
+            jax.ShapeDtypeStruct((ROWS, D), BF16),
         ),
         in_specs=[any_spec, any_spec, vmem_spec, vmem_spec, vmem_spec],
-        out_specs=(vmem_spec, any_spec, any_spec),
+        out_specs=(vmem_spec,) + (any_spec,) * 5,
         scratch_shapes=[
             vmem((4 * ROWS, D), BF16), vmem((4 * ROWS, D), BF16),
             parts, parts, parts, parts, parts, parts,
-            wide, wide, wide, wide, wide, wide, wide, wide,
+            wide, wide, wide, wide, wide,
             vmem((ROWS, 4 * ROWS), F32), vmem((ROWS, 4 * ROWS), F32), vmem((ROWS, S), F32),
             vmem((2, S, 4 * ROWS), BF16),
             vmem((ROWS, 4 * ROWS), BF16), vmem((ROWS, 4 * ROWS), BF16), vmem((4 * ROWS, 2 * ROWS), BF16),
@@ -572,8 +569,8 @@
             vmem((1, 2, S), F32), vmem((4, 2, S), F32),
             vmem((1, 2, S), F32), vmem((NY * NC, 2, S), F32),
             vmem((ROWS, 128), F32), vmem((ROWS, 128), F32), vmem((ROWS, 128), F32), vmem((ROWS, 128), F32),
-            vmem((ROWS, D), F32), vmem((ROWS, D), F32),
-            dma((2,)), dma((5,)), dma((2, 4, NCH)), dma((2, 4, NCH)), dma((2, NCH)), dma((2, NCH)),
+            wide, wide,
+            dma((2,)), dma((2,)), dma((2, 4, NCH)), dma((2, 4, NCH)), dma((2, NCH)), dma((2, NCH)),
             dma((4,)), dma((4,)), dma((4,)), dma((4,)), dma((4,)), dma((4,)), dma((2, 4, NCH)), dma((2, 4, NCH)), dma((2,)), dma((2,)), dma((3,)), dma((3,)),
             dma((6,)), dma((6,)),
         ],
@@ -588,11 +585,11 @@
     loss, gq, gp = pl.pallas_call(
         results,
         grid=(2,),
-        in_specs=[row, block, block],
+        in_specs=[row, block, block, block, block, block],
         out_specs=(row, block, block),
         out_shape=tuple(jax.ShapeDtypeStruct(a.shape, F32) for a in (loss, gq, gp)),
         name="results",
-    )(loss, gq, gp)
+    )(loss, gq, gp, up, dn, gx)
     return loss.reshape(ROWS), gq, gp
 
 

time: 142 us -> 141 us (level)
    pallas_call x1, Pallas kernels: 138 us -> 136 us  [on_device(): pl.pallas_call(functools.partial(kernel, NY, NC, D, shift), out_shape=(ja...]
where the time goes in v5:
time: 141 us; the launch traced here: 140 us
  Pallas kernels  140 us (99%)
    pallas_call x1, Pallas kernels, on_device(): pl.pallas_call(functools.partial(kernel, NY, NC, D, shift), out_shape=(ja...  136 us
    pallas_call x1, Pallas kernels, on_device(): pl.pallas_call(results, grid=(2,), in_specs=[row, block, block, block, bl...  4.18 us

profile of v5, /device:TPU:1, one launch (start us, length us, event | category | flops | bytes accessed | tf_op | source)
XLA Modules:
  0.0 140.4 jit_solution(17654579155295368796)
XLA Ops:
  0.6 135.6 %infonce.1 = (f32[1,128]{1,0:T(1,128)}, bf16[128,4096]{1,0:T(8,128)(2,1)}, bf16[128,4096]{1,0:T(8,128)(2,1)}, bf16[128,4096]{1,0:T(8,128)(2,1)}, bf16[128,4096]{1,0:T(8,128)(2,1)}, /*index=5*/bf16[128,4096]{1,0:T(8,128)(2,1)}) custom-call(bf16[128,4096]{1,0:T(8,128)(2,1)} %q_hbm.1, bf16[128,4096]{1,0:T(8,128)(2,1)} %p_hbm.1, s32[1,128]{1,0:T(1,128)} %pos_ref.1, ...), custom_call_target="tpu_custom_call" | custom-call | flops 8999999488 | bytes 8388608 | tf_op jit(solution)/shard_map/infonce/pallas_call | solution.py:546
  136.2 4.2 %results.1 = (f32[1,128]{1,0:T(1,128)}, f32[128,4096]{1,0:T(8,128)}, f32[128,4096]{1,0:T(8,128)}) custom-call(f32[1,128]{1,0:T(1,128)} %get-tuple-element.12.loss_in, bf16[128,4096]{1,0:T(8,128)(2,1)} %get-tuple-element.13.gq_in, bf16[128,4096]{1,0:T(8,128)(2,1)} %get-tuple-element.14.gp_in, bf16[128,4096]{1,0:T(8,128)(2,1)} %get-tuple-element.15.up_in, ...), custom_call_target="tpu_custom_call" | custom-call | tf_op jit(solution)/shard_map/results/pallas_call | solution.py:585
